TPU v7x, 32 devices: a whole 2x2x4 slice. The times are simulated.
32 devices in a mesh: seq: 8 (over z, x), rep: 4 (over y, core).
Axes of the slice: x: 2, y: 2, z: 4, core: 2. Of those that a mesh axis runs over, the one named last changes fastest.
Arguments:
- layer_incoming: bfloat16 [4, 2048, 1024], P('rep', 'seq'), may hold values from -6 to 6
- series_extents: int32 [4, 8], P('rep'), may hold values from 0 to 2048, as said below
- emitted_adjoint: bfloat16 [4, 2048, 1024], P('rep', 'seq'), may hold values from -6 to 6
- norm1_scaling: bfloat16 [1024], P(('seq', 'rep')), may hold values from 0.5 to 1.5
- norm1_offset: bfloat16 [1024], P(('seq', 'rep')), may hold values from -1.75 to 1.75
- mixer_lookup_portion: bfloat16 [1024], P(('seq', 'rep')), may hold values from 0 to 1
- mixer_payload_portion: bfloat16 [1024], P(('seq', 'rep')), may hold values from 0 to 1
- mixer_accept_portion: bfloat16 [1024], P(('seq', 'rep')), may hold values from 0 to 1
- temporal_fading_log: bfloat16 [1024], P(('seq', 'rep')), may hold values from -14 to -2
- present_step_reward: bfloat16 [1024], P(('seq', 'rep')), may hold values from -1 to 1
- mixer_lookup_matrix: bfloat16 [1024, 1024], P(('seq', 'rep')), may hold values from -0.1875 to 0.1875
- mixer_payload_matrix: bfloat16 [1024, 1024], P(('seq', 'rep')), may hold values from -0.1875 to 0.1875
- mixer_accept_matrix: bfloat16 [1024, 1024], P(('seq', 'rep')), may hold values from -0.1875 to 0.1875
- mixer_emit_matrix: bfloat16 [1024, 1024], P(('seq', 'rep')), may hold values from -1.5 to 1.5
- norm2_scaling: bfloat16 [1024], P(('seq', 'rep')), may hold values from 0.5 to 1.5
- norm2_offset: bfloat16 [1024], P(('seq', 'rep')), may hold values from -1.75 to 1.75
- feedforward_lookup_portion: bfloat16 [1024], P(('seq', 'rep')), may hold values from 0 to 1
- feedforward_accept_portion: bfloat16 [1024], P(('seq', 'rep')), may hold values from 0 to 1
- feedforward_lookup_matrix: bfloat16 [1024, 4096], P(('seq', 'rep')), may hold values from -0.1875 to 0.1875
- feedforward_payload_matrix: bfloat16 [4096, 1024], P(('seq', 'rep')), may hold values from -0.09375 to 0.09375
- feedforward_accept_matrix: bfloat16 [1024, 1024], P(('seq', 'rep')), may hold values from -0.1875 to 0.1875
Outputs:
- block_output: bfloat16 [4, 2048, 1024], P('rep', 'seq')
- input_grad: float32 [4, 2048, 1024], P('rep', 'seq')
- ln1_gain_grad: float32 [1024], P(('seq', 'rep'))
- ln1_bias_grad: float32 [1024], P(('seq', 'rep'))
- att_mix_k_grad: float32 [1024], P(('seq', 'rep'))
- att_mix_v_grad: float32 [1024], P(('seq', 'rep'))
- att_mix_r_grad: float32 [1024], P(('seq', 'rep'))
- time_decay_grad: float32 [1024], P(('seq', 'rep'))
- time_first_grad: float32 [1024], P(('seq', 'rep'))
- att_key_grad: float32 [1024, 1024], P(('seq', 'rep'))
- att_value_grad: float32 [1024, 1024], P(('seq', 'rep'))
- att_receptance_grad: float32 [1024, 1024], P(('seq', 'rep'))
- att_output_grad: float32 [1024, 1024], P(('seq', 'rep'))
- ln2_gain_grad: float32 [1024], P(('seq', 'rep'))
- ln2_bias_grad: float32 [1024], P(('seq', 'rep'))
- ffn_mix_k_grad: float32 [1024], P(('seq', 'rep'))
- ffn_mix_r_grad: float32 [1024], P(('seq', 'rep'))
- ffn_key_grad: float32 [1024, 4096], P(('seq', 'rep'))
- ffn_value_grad: float32 [4096, 1024], P(('seq', 'rep'))
- ffn_receptance_grad: float32 [1024, 1024], P(('seq', 'rep'))
Inputs may be any that keep to these rules, and one draw needn't show every extreme that they name: `series_extents`: row g lists, in order, the lengths of the sequences that lie end to end over the 2048 tokens of group g, each 256, 1024 or 2048, followed by zeros; they sum to 2048, and at least one is 2048.
All inputs are finite; a program needn't handle non-finite values.
Results may differ from a plain program's by a relative error of at most 0.014.
Values may be sent and summed in bfloat16 or wider, within the bound.
No kernel may reach another device: no remote copies, remote signals or barrier semaphores. Data moves between devices by JAX's collectives and lax.ppermute only.
A program may use at most 192 MiB of HBM per device.

v0:
```python
from functools import partial
import math

import jax
import jax.numpy as jnp
from jax import lax
from jax.sharding import PartitionSpec as P

EPSILON = 1e-05


def from_behind(block, axis, distance):
    devices = range(lax.axis_size(axis))
    route = [(i - distance, i) for i in devices if i - distance in devices]
    return lax.ppermute(block, axis, route)


def layer_norm(inputs, gain, bias):
    center = jnp.mean(inputs, axis=-1, keepdims=True)
    deviation = inputs - center
    variance = jnp.mean(deviation * deviation, axis=-1, keepdims=True)
    return deviation * lax.rsqrt(variance + EPSILON) * gain + bias


def mix_rows(retain_mask, normed, previous, factors):
    shifted = jnp.concatenate([previous, normed[:-1]], axis=0) * retain_mask[:, None]
    return tuple((normed * factor + shifted * (1.0 - factor) for factor in factors))


def combine_state(earlier, later):
    return (
        earlier[0] * later[0],
        later[0] * earlier[1] + later[1],
        later[0] * earlier[2] + later[2],
    )


def nearby_fragments(
    retain_mask, lookup_rows, payload_rows, temporal_fading_log, present_step_reward
):
    rows, breadth_count = lookup_rows.shape
    span_length = math.gcd(rows, 128)
    block_list = rows // span_length
    rate = jnp.exp(temporal_fading_log)
    reward_array = jnp.exp(present_step_reward)
    scaling_coefficient = jnp.exp(lookup_rows)
    multiplied_piece = scaling_coefficient * payload_rows
    segment = jnp.cumsum((1.0 - retain_mask).reshape(block_list, span_length), axis=1)
    place = jnp.arange(span_length, dtype=jnp.float32)
    lower = place[None, :] < place[:, None]
    linked = jnp.logical_and(lower[None], segment[:, :, None] == segment[:, None, :]).astype(
        jnp.float32
    )
    rise = jnp.exp(place[:, None] * rate[None, :])
    fall = jnp.exp(-(place[:, None] - 1.0) * rate[None, :])
    num_terms = multiplied_piece.reshape(block_list, span_length, breadth_count) * rise[None]
    den_terms = scaling_coefficient.reshape(block_list, span_length, breadth_count) * rise[None]
    within_dividend = (
        jnp.einsum("bti,bic->btc", linked, num_terms, precision=lax.Precision.HIGHEST) * fall[None]
    )
    within_divisor = (
        jnp.einsum("bti,bic->btc", linked, den_terms, precision=lax.Precision.HIGHEST) * fall[None]
    )
    within_dividend = within_dividend + reward_array * multiplied_piece.reshape(
        block_list, span_length, breadth_count
    )
    within_divisor = within_divisor + reward_array * scaling_coefficient.reshape(
        block_list, span_length, breadth_count
    )
    last_same = (segment == segment[:, -1:]).astype(jnp.float32)
    end_fall = jnp.exp(-(span_length - 1.0) * rate)
    end_num = (
        jnp.einsum("bi,bic->bc", last_same, num_terms, precision=lax.Precision.HIGHEST)
        * end_fall[None]
    )
    end_den = (
        jnp.einsum("bi,bic->bc", last_same, den_terms, precision=lax.Precision.HIGHEST)
        * end_fall[None]
    )
    untouched = (segment == 0.0).astype(jnp.float32)
    block_pass = untouched[:, -1:] * jnp.exp(-span_length * rate)[None, :]
    total_pass, total_num, total_den = lax.associative_scan(
        combine_state, (block_pass, end_num, end_den)
    )
    enter_pass = jnp.concatenate([jnp.ones_like(total_pass[:1]), total_pass[:-1]], axis=0)
    enter_num = jnp.concatenate([jnp.zeros_like(total_num[:1]), total_num[:-1]], axis=0)
    enter_den = jnp.concatenate([jnp.zeros_like(total_den[:1]), total_den[:-1]], axis=0)
    reach_block = untouched[:, :, None] * jnp.exp(-place[:, None] * rate[None, :])[None]
    num_base = (within_dividend + reach_block * enter_num[:, None, :]).reshape(rows, breadth_count)
    den_base = (within_divisor + reach_block * enter_den[:, None, :]).reshape(rows, breadth_count)
    reach = (reach_block * enter_pass[:, None, :]).reshape(rows, breadth_count)
    return (num_base, den_base, reach, total_pass[-1], total_num[-1], total_den[-1])


def feature_recurrent_average(
    retain_mask, lookup_rows, payload_rows, temporal_fading_log, present_step_reward
):
    fragments = nearby_fragments(
        retain_mask, lookup_rows, payload_rows, temporal_fading_log, present_step_reward
    )
    return fragments[0] / fragments[1]


def keep_rows(positions, lengths):
    begins = jnp.cumsum(lengths) - lengths
    starting = jnp.any(positions[:, None] == begins[None, :], axis=1)
    return jnp.where(starting, 0.0, 1.0).astype(jnp.float32)


def times_back(grad_rows, weight_full):
    return jnp.einsum("tf,df->td", grad_rows, weight_full, preferred_element_type=jnp.float32)


def outer_sum(left_rows, right_rows):
    return jnp.einsum("td,tf->df", left_rows, right_rows, preferred_element_type=jnp.float32)


def fold_return(grad_rows, returned):
    return jnp.concatenate([grad_rows[:-1], grad_rows[-1:] + returned], axis=0)


def per_device(
    layer_incoming,
    series_extents,
    emitted_adjoint,
    norm1_scaling,
    norm1_offset,
    mixer_lookup_portion,
    mixer_payload_portion,
    mixer_accept_portion,
    temporal_fading_log,
    present_step_reward,
    mixer_lookup_matrix,
    mixer_payload_matrix,
    mixer_accept_matrix,
    mixer_emit_matrix,
    norm2_scaling,
    norm2_offset,
    feedforward_lookup_portion,
    feedforward_accept_portion,
    feedforward_lookup_matrix,
    feedforward_payload_matrix,
    feedforward_accept_matrix,
):
    gathered = (
        lax.all_gather(norm1_scaling, ("seq", "rep"), axis=0, tiled=True),
        lax.all_gather(norm1_offset, ("seq", "rep"), axis=0, tiled=True),
        lax.all_gather(mixer_lookup_portion, ("seq", "rep"), axis=0, tiled=True),
        lax.all_gather(mixer_payload_portion, ("seq", "rep"), axis=0, tiled=True),
        lax.all_gather(mixer_accept_portion, ("seq", "rep"), axis=0, tiled=True),
        lax.all_gather(temporal_fading_log, ("seq", "rep"), axis=0, tiled=True),
        lax.all_gather(present_step_reward, ("seq", "rep"), axis=0, tiled=True),
        lax.all_gather(mixer_lookup_matrix, ("seq", "rep"), axis=0, tiled=True),
        lax.all_gather(mixer_payload_matrix, ("seq", "rep"), axis=0, tiled=True),
        lax.all_gather(mixer_accept_matrix, ("seq", "rep"), axis=0, tiled=True),
        lax.all_gather(mixer_emit_matrix, ("seq", "rep"), axis=0, tiled=True),
        lax.all_gather(norm2_scaling, ("seq", "rep"), axis=0, tiled=True),
        lax.all_gather(norm2_offset, ("seq", "rep"), axis=0, tiled=True),
        lax.all_gather(feedforward_lookup_portion, ("seq", "rep"), axis=0, tiled=True),
        lax.all_gather(feedforward_accept_portion, ("seq", "rep"), axis=0, tiled=True),
        lax.all_gather(feedforward_lookup_matrix, ("seq", "rep"), axis=0, tiled=True),
        lax.all_gather(feedforward_payload_matrix, ("seq", "rep"), axis=0, tiled=True),
        lax.all_gather(feedforward_accept_matrix, ("seq", "rep"), axis=0, tiled=True),
    )
    (
        full_ln1_gain,
        full_ln1_bias,
        full_mix_k,
        full_mix_v,
        full_mix_r,
        full_decay,
        entire_initial,
        full_att_key,
        full_att_value,
        full_att_recept,
        full_att_output,
        full_ln2_gain,
        full_ln2_bias,
        full_ffn_mix_k,
        full_ffn_mix_r,
        full_ffn_key,
        full_ffn_value,
        full_ffn_recept,
    ) = gathered
    array_operand = lambda element_item: element_item.astype(jnp.float32)
    inputs = layer_incoming[0].astype(jnp.float32)
    cotangent = emitted_adjoint[0].astype(jnp.float32)
    rows, breadth_count = inputs.shape
    parts = lax.axis_size("seq")
    lengths = series_extents[0]
    positions = lax.axis_index("seq") * rows + jnp.arange(rows, dtype=jnp.int32)
    retain_mask = keep_rows(positions, lengths)
    mixer = partial(mix_rows, retain_mask)
    decay_full = array_operand(full_decay)
    reward_whole = array_operand(entire_initial)
    normed, norm_pull = jax.vjp(
        layer_norm, inputs, array_operand(full_ln1_gain), array_operand(full_ln1_bias)
    )
    previous = from_behind(normed[-1:], "seq", 1)
    (mixed_key, mixed_value, mixed_recept), mix_pull = jax.vjp(
        mixer,
        normed,
        previous,
        (array_operand(full_mix_k), array_operand(full_mix_v), array_operand(full_mix_r)),
    )
    low_key = mixed_key.astype(jnp.bfloat16)
    low_value = mixed_value.astype(jnp.bfloat16)
    low_recept = mixed_recept.astype(jnp.bfloat16)
    lookup_rows = jnp.dot(low_key, full_att_key, preferred_element_type=jnp.float32).astype(
        jnp.bfloat16
    )
    payload_rows = jnp.dot(low_value, full_att_value, preferred_element_type=jnp.float32).astype(
        jnp.bfloat16
    )
    recept = jax.nn.sigmoid(
        jnp.dot(low_recept, full_att_recept, preferred_element_type=jnp.float32)
    )
    chan_keys, chan_values = (
        lax.all_to_all(lookup_rows, "seq", split_axis=1, concat_axis=0, tiled=True),
        lax.all_to_all(payload_rows, "seq", split_axis=1, concat_axis=0, tiled=True),
    )
    portion_quantity = breadth_count // parts
    foremost_feature = lax.axis_index("seq") * portion_quantity
    decay_part = lax.dynamic_slice_in_dim(decay_full, foremost_feature, portion_quantity)
    reward_portion = lax.dynamic_slice_in_dim(reward_whole, foremost_feature, portion_quantity)
    group_keep = keep_rows(jnp.arange(chan_keys.shape[0], dtype=jnp.int32), lengths)
    chan_out, weighted_key_value_pullback = jax.vjp(
        partial(feature_recurrent_average, group_keep),
        chan_keys.astype(jnp.float32),
        chan_values.astype(jnp.float32),
        decay_part,
        reward_portion,
    )
    scaled_combination = lax.all_to_all(
        chan_out.astype(jnp.bfloat16), "seq", split_axis=0, concat_axis=1, tiled=True
    )
    gated = (recept * scaled_combination.astype(jnp.float32)).astype(jnp.bfloat16)
    middle = inputs + jnp.dot(gated, full_att_output, preferred_element_type=jnp.float32)
    normed2, norm2_pull = jax.vjp(
        layer_norm, middle, array_operand(full_ln2_gain), array_operand(full_ln2_bias)
    )
    previous2 = from_behind(normed2[-1:], "seq", 1)
    (ffn_in_key, ffn_in_recept), mix2_pull = jax.vjp(
        mixer, normed2, previous2, (array_operand(full_ffn_mix_k), array_operand(full_ffn_mix_r))
    )
    low_ffn_key = ffn_in_key.astype(jnp.bfloat16)
    low_ffn_recept = ffn_in_recept.astype(jnp.bfloat16)
    pre_hidden = jnp.dot(low_ffn_key, full_ffn_key, preferred_element_type=jnp.float32)
    hidden = jnp.square(jax.nn.relu(pre_hidden)).astype(jnp.bfloat16)
    value_out = jnp.dot(hidden, full_ffn_value, preferred_element_type=jnp.float32)
    gate = jax.nn.sigmoid(
        jnp.dot(low_ffn_recept, full_ffn_recept, preferred_element_type=jnp.float32)
    )
    block_output = (middle + gate * value_out).astype(jnp.bfloat16)
    d_value_out = (cotangent * gate).astype(jnp.bfloat16)
    d_gate_pre = (cotangent * value_out * gate * (1.0 - gate)).astype(jnp.bfloat16)
    d_hidden = times_back(d_value_out, full_ffn_value)
    d_pre_hidden = (d_hidden * 2.0 * jax.nn.relu(pre_hidden)).astype(jnp.bfloat16)
    grad_ffn_value = outer_sum(hidden, d_value_out)
    grad_ffn_key = outer_sum(low_ffn_key, d_pre_hidden)
    grad_ffn_recept = outer_sum(low_ffn_recept, d_gate_pre)
    d_ffn_key_in = times_back(d_pre_hidden, full_ffn_key)
    d_ffn_recept_in = times_back(d_gate_pre, full_ffn_recept)
    d_normed2, d_previous2, ffn_mix_grads = mix2_pull((d_ffn_key_in, d_ffn_recept_in))
    returned2 = from_behind(d_previous2, "seq", -1)
    d_middle_norm, grad_ln2_gain, grad_ln2_bias = norm2_pull(fold_return(d_normed2, returned2))
    d_middle = cotangent + d_middle_norm
    key_sums = (
        lax.psum_scatter(grad_ln2_gain, ("seq", "rep"), scatter_dimension=0, tiled=True),
        lax.psum_scatter(grad_ln2_bias, ("seq", "rep"), scatter_dimension=0, tiled=True),
        lax.psum_scatter(ffn_mix_grads[0], ("seq", "rep"), scatter_dimension=0, tiled=True),
        lax.psum_scatter(ffn_mix_grads[1], ("seq", "rep"), scatter_dimension=0, tiled=True),
        lax.psum_scatter(grad_ffn_key, ("seq", "rep"), scatter_dimension=0, tiled=True),
    )
    value_summed = lax.psum_scatter(grad_ffn_value, ("seq", "rep"), scatter_dimension=0, tiled=True)
    recept_summed = lax.psum_scatter(
        grad_ffn_recept, ("seq", "rep"), scatter_dimension=0, tiled=True
    )
    d_attended = d_middle.astype(jnp.bfloat16)
    grad_att_output = outer_sum(gated, d_attended)
    d_gated = times_back(d_attended, full_att_output)
    d_weighted = (d_gated * recept).astype(jnp.bfloat16)
    d_recept_pre = (
        d_gated * scaled_combination.astype(jnp.float32) * recept * (1.0 - recept)
    ).astype(jnp.bfloat16)
    chan_grad = lax.all_to_all(d_weighted, "seq", split_axis=1, concat_axis=0, tiled=True)
    (
        feature_lookup_derivative,
        feature_payload_derivative,
        fading_portion_derivative,
        reward_portion_derivative,
    ) = weighted_key_value_pullback(chan_grad.astype(jnp.float32))
    d_keys, d_values = (
        lax.all_to_all(
            feature_lookup_derivative.astype(jnp.bfloat16),
            "seq",
            split_axis=0,
            concat_axis=1,
            tiled=True,
        ),
        lax.all_to_all(
            feature_payload_derivative.astype(jnp.bfloat16),
            "seq",
            split_axis=0,
            concat_axis=1,
            tiled=True,
        ),
    )
    grad_decay = lax.dynamic_update_slice_in_dim(
        jnp.zeros((breadth_count,), jnp.float32), fading_portion_derivative, foremost_feature, 0
    )
    reward_derivative = lax.dynamic_update_slice_in_dim(
        jnp.zeros((breadth_count,), jnp.float32), reward_portion_derivative, foremost_feature, 0
    )
    grad_att_key = outer_sum(low_key, d_keys)
    grad_att_value = outer_sum(low_value, d_values)
    grad_att_recept = outer_sum(low_recept, d_recept_pre)
    d_mixed_key = times_back(d_keys, full_att_key)
    d_mixed_value = times_back(d_values, full_att_value)
    d_mixed_recept = times_back(d_recept_pre, full_att_recept)
    d_normed, d_previous, att_mix_grads = mix_pull((d_mixed_key, d_mixed_value, d_mixed_recept))
    returned = from_behind(d_previous, "seq", -1)
    d_inputs_norm, grad_ln1_gain, grad_ln1_bias = norm_pull(fold_return(d_normed, returned))
    input_grad = d_middle + d_inputs_norm
    time_sums = (
        lax.psum_scatter(grad_ln1_gain, ("seq", "rep"), scatter_dimension=0, tiled=True),
        lax.psum_scatter(grad_ln1_bias, ("seq", "rep"), scatter_dimension=0, tiled=True),
        lax.psum_scatter(att_mix_grads[0], ("seq", "rep"), scatter_dimension=0, tiled=True),
        lax.psum_scatter(att_mix_grads[1], ("seq", "rep"), scatter_dimension=0, tiled=True),
        lax.psum_scatter(att_mix_grads[2], ("seq", "rep"), scatter_dimension=0, tiled=True),
        lax.psum_scatter(grad_decay, ("seq", "rep"), scatter_dimension=0, tiled=True),
        lax.psum_scatter(reward_derivative, ("seq", "rep"), scatter_dimension=0, tiled=True),
        lax.psum_scatter(grad_att_key, ("seq", "rep"), scatter_dimension=0, tiled=True),
        lax.psum_scatter(grad_att_value, ("seq", "rep"), scatter_dimension=0, tiled=True),
        lax.psum_scatter(grad_att_recept, ("seq", "rep"), scatter_dimension=0, tiled=True),
        lax.psum_scatter(grad_att_output, ("seq", "rep"), scatter_dimension=0, tiled=True),
    )
    return (
        block_output[None],
        input_grad[None],
        time_sums[0],
        time_sums[1],
        time_sums[2],
        time_sums[3],
        time_sums[4],
        time_sums[5],
        time_sums[6],
        time_sums[7],
        time_sums[8],
        time_sums[9],
        time_sums[10],
        key_sums[0],
        key_sums[1],
        key_sums[2],
        key_sums[3],
        key_sums[4],
        value_summed,
        recept_summed,
    )


def solution(mesh):
    return jax.shard_map(
        per_device,
        mesh=mesh,
        in_specs=(
            P("rep", "seq", None),
            P("rep", None),
            P("rep", "seq", None),
            P(("seq", "rep")),
            P(("seq", "rep")),
            P(("seq", "rep")),
            P(("seq", "rep")),
            P(("seq", "rep")),
            P(("seq", "rep")),
            P(("seq", "rep")),
            P(("seq", "rep"), None),
            P(("seq", "rep"), None),
            P(("seq", "rep"), None),
            P(("seq", "rep"), None),
            P(("seq", "rep")),
            P(("seq", "rep")),
            P(("seq", "rep")),
            P(("seq", "rep")),
            P(("seq", "rep"), None),
            P(("seq", "rep"), None),
            P(("seq", "rep"), None),
        ),
        out_specs=(
            P("rep", "seq", None),
            P("rep", "seq", None),
            P(("seq", "rep")),
            P(("seq", "rep")),
            P(("seq", "rep")),
            P(("seq", "rep")),
            P(("seq", "rep")),
            P(("seq", "rep")),
            P(("seq", "rep")),
            P(("seq", "rep"), None),
            P(("seq", "rep"), None),
            P(("seq", "rep"), None),
            P(("seq", "rep"), None),
            P(("seq", "rep")),
            P(("seq", "rep")),
            P(("seq", "rep")),
            P(("seq", "rep")),
            P(("seq", "rep"), None),
            P(("seq", "rep"), None),
            P(("seq", "rep"), None),
        ),
        check_vma=False,
    )
```

profile of v0, /device:TPU:0, one launch (start us, length us, event | category | flops | bytes accessed | tf_op | source)
XLA Modules:
  0.0 1558.4 jit_solution(2097810470801142493)
XLA Ops:
  21.1 42.8 %all-reduce.89 = (bf16[1024]{0:T(1024)(128)(2,1)S(1)}, bf16[1024]{0:T(1024)(128)(2,1)S(1)}, bf16[1024]{0:T(1024)(128)(2,1)S(1)}, bf16[1024]{0:T(1024)(128)(2,1)S...) all-reduce(bf16[1024]{0:T(1024)(128)(2,1)S(1)} %dynamic-update-slic, ...), channel_id=1, replica_groups=mesh['seq'=8,'rep'=4] {'seq','rep'}, use_global_device_ids=true, to_apply=%add.68 | all-reduce | flops 11264 | bytes 45056
  64.0 1.2 convert_reduce_fusion
  65.2 1.3 fusion.19
  66.8 4.2 collective-permute-start
  71.3 1.2 slice_bitcast_fusion
  72.7 2.8 fusion.14
  76.4 4.7 all-to-all-start.1
  81.9 49.1 %all-gather.10.cloned.1.call-done = bf16[1024,1024]{1,0:T(8,128)(2,1)} async-done(((bf16[32,1024]{1,0:T(8,128)(2,1)}), bf16[1024,1024]{1,0:T(8,128)(2,1)}) %all-gather.10.cloned.1.call-update) | async-done | bytes 2097168 | tf_op jit(solution)/shard_map/all_gather | solution.py:153
  131.1 2.5 fusion.13
  134.5 4.3 all-to-all-start
  140.3 14.8 all-to-all-done
  159.8 1.3 fusion.47
  161.2 2.9 divide_convert_fusion
  164.1 3.7 all-to-all-start.2
  168.3 25.2 %all-gather.8.cloned.1.call-done = bf16[1024,1024]{1,0:T(8,128)(2,1)} async-done(((bf16[32,1024]{1,0:T(8,128)(2,1)}), bf16[1024,1024]{1,0:T(8,128)(2,1)}) %all-gather.8.cloned.1.call-update) | async-done | bytes 2097168 | tf_op jit(solution)/shard_map/all_gather | solution.py:155
  193.6 4.1 fusion.38
  197.7 53.9 %all-gather.14.cloned.1.call-done = bf16[1024,1024]{1,0:T(8,128)(2,1)} async-done(((bf16[32,1024]{1,0:T(8,128)(2,1)}), bf16[1024,1024]{1,0:T(8,128)(2,1)}) %all-gather.14.cloned.1.call-update) | async-done | bytes 2097168 | tf_op jit(solution)/shard_map/all_gather | solution.py:156
  251.6 2.4 fusion.139
  254.5 3.3 collective-permute-start.1
  257.9 1.2 collective-permute-done.1
  259.2 1.4 add_convert_fusion.1
  260.6 49.0 %all-gather.16.cloned.1.call-done = bf16[1024,1024]{1,0:T(8,128)(2,1)} async-done(((bf16[32,1024]{1,0:T(8,128)(2,1)}), bf16[1024,1024]{1,0:T(8,128)(2,1)}) %all-gather.16.cloned.1.call-update) | async-done | bytes 2097168 | tf_op jit(solution)/shard_map/all_gather | solution.py:163
  309.5 3.4 fusion.7
  312.9 75.8 %all-gather.18.cloned.1.call-done = bf16[1024,4096]{1,0:T(8,128)(2,1)} async-done(((bf16[32,4096]{1,0:T(8,128)(2,1)}), bf16[1024,4096]{1,0:T(8,128)(2,1)}) %all-gather.18.cloned.1.call-update) | async-done | bytes 8388624 | tf_op jit(solution)/shard_map/all_gather | solution.py:161
  388.7 8.0 convolution_maximum_fusion
  396.7 71.1 %all-gather.20.cloned.1.call-done = bf16[4096,1024]{1,0:T(8,128)(2,1)} async-done(((bf16[128,1024]{1,0:T(8,128)(2,1)}), bf16[4096,1024]{1,0:T(8,128)(2,1)}) %all-gather.20.cloned.1.call-update) | async-done | bytes 8388624 | tf_op jit(solution)/shard_map/all_gather | solution.py:162
  467.8 8.2 fusion.32
  476.7 2.8 fusion.146
  479.8 7.3 fusion.1
  487.1 6.5 fusion.140
  493.7 1.7 multiply_reduce_fusion.1
  495.6 1.3 collective-permute-start.2
  498.0 3.1 collective-permute-done.2
  505.5 1.1 fusion.41
  506.6 3.1 fusion.121
  509.7 2.0 copy.99
  511.7 4.9 all-to-all-start.3
  516.6 2.7 fusion.144
  519.7 13.0 all-to-all-done.3
  532.6 1.2 convert_element_type.232
  534.0 4.1 multiply_reduce_fusion.11
  544.6 4.2 multiply_reduce_fusion.5
  548.8 2.0 multiply_reduce_fusion.6
  550.9 1.2 fusion.44
  552.0 19.6 %all_to_all.81 = bf16[8,256,128]{2,1,0:T(8,128)(2,1)S(1)} all-to-all(bf16[8,256,128]{2,1,0:T(8,128)(2,1)S(1)} %get-tuple-element.102), channel_id=1, replica_groups=mesh['seq'=8,'rep'=4] {'seq'}, dimensions={0} | all-to-all | bytes 1048576 | tf_op jit(solution)/shard_map/all_to_all | solution.py:294
  571.8 3.1 fusion.62
  575.9 18.1 %all_to_all.82 = bf16[8,256,128]{2,1,0:T(8,128)(2,1)S(1)} all-to-all(bf16[8,256,128]{2,1,0:T(8,128)(2,1)S(1)} %copy-done.41), channel_id=1, replica_groups=mesh['seq'=8,'rep'=4] {'seq'}, dimensions={0} | all-to-all | bytes 1048576 | tf_op jit(solution)/shard_map/all_to_all | solution.py:301
  594.3 3.0 fusion.60
  597.4 1.5 copy-done.14
  598.9 9.2 fusion.145
  609.3 10.3 fusion.55
  622.2 2.3 fusion.142
  628.0 2.3 fusion.143
  631.4 1.3 collective-permute-start.3
  633.4 3.6 collective-permute-done.3
  637.0 1.1 multiply_reduce_fusion.13
  638.8 39.9 %all-reduce.88 = (f32[1024]{0:T(1024)S(1)}, f32[1024]{0:T(1024)S(1)}, f32[1024]{0:T(1024)S(1)}, f32[1024]{0:T(1024)S(1)}, f32[1024]{0:T(1024)S(1)}, /*index=5*/f...) all-reduce(f32[1024]{0:T(1024)S(1)} %get-tuple-element.22, ...), channel_id=2, replica_groups=mesh['seq'=8,'rep'=4] {'seq','rep'}, use_global_device_ids=true, to_apply=%region_15.16.clone | all-reduce | flops 11264 | bytes 90112
  685.1 1.5 add_bitcast_fusion
  686.5 76.3 %reduce-scatter.12.cloned.1.call-done = f32[32,1024]{1,0:T(8,128)} async-done(((f32[1024,1024]{1,0:T(8,128)}), f32[32,1024]{1,0:T(8,128)}) %reduce-scatter.12.cloned.1.call-update) | async-done | bytes 131088 | tf_op jit(solution)/shard_map/reduce_scatter | solution.py:335
  762.8 139.8 %reduce-scatter.14.cloned.1.call-done = f32[32,1024]{1,0:T(8,128)} async-done(((f32[1024,1024]{1,0:T(8,128)}), f32[32,1024]{1,0:T(8,128)}) %reduce-scatter.14.cloned.1.call-update) | async-done | bytes 131088 | tf_op jit(solution)/shard_map/reduce_scatter | solution.py:336
  902.6 139.9 %reduce-scatter.8.cloned.1.call-done = f32[32,1024]{1,0:T(8,128)} async-done(((f32[1024,1024]{1,0:T(8,128)}), f32[32,1024]{1,0:T(8,128)}) %reduce-scatter.8.cloned.1.call-update) | async-done | bytes 131088 | tf_op jit(solution)/shard_map/reduce_scatter | solution.py:333
  1042.5 139.8 %reduce-scatter.10.cloned.1.call-done = f32[32,1024]{1,0:T(8,128)} async-done(((f32[1024,1024]{1,0:T(8,128)}), f32[32,1024]{1,0:T(8,128)}) %reduce-scatter.10.cloned.1.call-update) | async-done | bytes 131088 | tf_op jit(solution)/shard_map/reduce_scatter | solution.py:334
  1182.3 181.8 %reduce-scatter.16.cloned.1.call-done = f32[32,4096]{1,0:T(8,128)} async-done(((f32[1024,4096]{1,0:T(8,128)}), f32[32,4096]{1,0:T(8,128)}) %reduce-scatter.16.cloned.1.call-update) | async-done | bytes 524304 | tf_op jit(solution)/shard_map/reduce_scatter | solution.py:273
  1364.1 187.3 %reduce-scatter.18.cloned.1.call-done = f32[128,1024]{1,0:T(8,128)} async-done(((f32[4096,1024]{1,0:T(8,128)}), f32[128,1024]{1,0:T(8,128)}) %reduce-scatter.18.cloned.1.call-update) | async-done | bytes 524304 | tf_op jit(solution)/shard_map/reduce_scatter | solution.py:275
  (463 shorter events, 54.7 us)
Async XLA Ops:
  7.2 59.3 %copy-start = (bf16[1,256,1024]{2,1,0:T(8,128)(2,1)S(1)}, bf16[1,256,1024]{2,1,0:T(8,128)(2,1)}, u32[]{:S(2)}) copy-start(bf16[1,256,1024]{2,1,0:T(8,128)(2,1)} %param.21) | copy-start | bytes 1572868
  7.2 63.8 %copy-start.91 = (s32[1,8]{1,0:T(1,128)S(1)}, s32[1,8]{1,0:T(1,128)}, u32[]{:S(2)}) copy-start(s32[1,8]{1,0:T(1,128)} %param.22) | copy-start | bytes 100
  7.2 65.5 %all-gather.12.cloned.1.call-start = ((), (), s32[]{:S(2)}) async-start(), calls=%async_computation.15 | async-start | bytes 2162688 | tf_op jit(solution)/shard_map/all_gather | solution.py:154
  7.9 123.1 %all-gather.10.cloned.1.call-start = ((), (), s32[]{:S(2)}) async-start(), calls=%async_computation.14 | async-start | bytes 2162688 | tf_op jit(solution)/shard_map/all_gather | solution.py:153
  8.7 184.9 %all-gather.8.cloned.1.call-start = ((), (), s32[]{:S(2)}) async-start(), calls=%async_computation.13 | async-start | bytes 2162688 | tf_op jit(solution)/shard_map/all_gather | solution.py:155
  9.4 242.1 %all-gather.14.cloned.1.call-start = ((), (), s32[]{:S(2)}) async-start(), calls=%async_computation.16 | async-start | bytes 2162688 | tf_op jit(solution)/shard_map/all_gather | solution.py:156
  10.0 299.5 %all-gather.16.cloned.1.call-start = ((), (), s32[]{:S(2)}) async-start(), calls=%async_computation.17 | async-start | bytes 2162688 | tf_op jit(solution)/shard_map/all_gather | solution.py:163
  10.6 378.1 %all-gather.18.cloned.1.call-start = ((), (), s32[]{:S(2)}) async-start(), calls=%async_computation.18 | async-start | bytes 8650752 | tf_op jit(solution)/shard_map/all_gather | solution.py:161
  11.2 456.6 %all-gather.20.cloned.1.call-start = ((), (), s32[]{:S(2)}) async-start(), calls=%async_computation.19 | async-start | bytes 8650752 | tf_op jit(solution)/shard_map/all_gather | solution.py:162
  66.5 6.1 copy-start.62
  66.8 5.8 collective-permute-start
  72.6 58.5 %copy-start.5 = (f32[255,1024]{1,0:T(8,128)}, f32[255,1024]{1,0:T(8,128)S(1)}, u32[]{:S(2)}) copy-start(f32[255,1024]{1,0:T(8,128)S(1)} %get-tuple-element.104) | copy-start | bytes 3133444
  76.4 58.1 %all-to-all-start.1 = ((bf16[256,8,128]{2,0,1:T(8,128)(2,1)}), bf16[256,8,128]{2,0,1:T(8,128)(2,1)S(1)}, u32[]{:S(2)}, u32[]{:S(2)}) async-start(bf16[256,8,128]{2,0,1:T(8,128)(2,1)} %bitcast.175), calls=%async_computation.1 | async-start | bytes 1048576 | tf_op jit(solution)/shard_map/all_to_all | solution.py:220
  81.5 57.6 %copy-start.77 = (f32[128]{0:T(128)}, f32[128]{0:T(128)S(1)}, u32[]{:S(2)}) copy-start(f32[128]{0:T(128)S(1)} %get-tuple-element.91) | copy-start | bytes 1540
  81.5 57.6 %copy-start.83 = (f32[128]{0:T(128)}, f32[128]{0:T(128)S(1)}, u32[]{:S(2)}) copy-start(f32[128]{0:T(128)S(1)} %get-tuple-element.189) | copy-start | bytes 1540
  81.9 56.9 %copy-start.84 = (f32[16]{0:T(128)}, f32[16]{0:T(128)S(1)}, u32[]{:S(2)}) copy-start(f32[16]{0:T(128)S(1)} %slice_reduce_fusion) | copy-start | bytes 196
  134.5 20.7 %copy-start.17 = (bf16[256,8,128]{2,0,1:T(8,128)(2,1)}, bf16[256,8,128]{2,0,1:T(8,128)(2,1)S(1)}, u32[]{:S(2)}) copy-start(bf16[256,8,128]{2,0,1:T(8,128)(2,1)S(1)} %all-to-all-done.1) | copy-start | bytes 1572868
  134.5 20.6 %all-to-all-start = ((bf16[256,8,128]{2,0,1:T(8,128)(2,1)}), bf16[256,8,128]{2,0,1:T(8,128)(2,1)S(1)}, u32[]{:S(2)}, u32[]{:S(2)}) async-start(bf16[256,8,128]{2,0,1:T(8,128)(2,1)} %bitcast.176), calls=%async_computation | async-start | bytes 1048576 | tf_op jit(solution)/shard_map/all_to_all | solution.py:219
  138.9 17.7 %copy-start.82 = (f32[1024]{0:T(1024)}, f32[1024]{0:T(1024)S(1)}, u32[]{:S(2)}) copy-start(f32[1024]{0:T(1024)S(1)} %convert_element_type.191) | copy-start | bytes 12292
  138.9 17.7 %copy-start.89 = (f32[128]{0:T(128)}, f32[128]{0:T(128)S(1)}, u32[]{:S(2)}) copy-start(f32[128]{0:T(128)S(1)} %add_negate_fusion) | copy-start | bytes 1540
  139.0 22.2 %copy-start.85 = (f32[128]{0:T(128)}, f32[128]{0:T(128)S(1)}, u32[]{:S(2)}) copy-start(f32[128]{0:T(128)S(1)} %dynamic-slice_exponential_fusion) | copy-start | bytes 1540
  139.1 18.8 %copy-start.90 = (f32[128]{0:T(128)}, f32[128]{0:T(128)S(1)}, u32[]{:S(2)}) copy-start(f32[128]{0:T(128)S(1)} %multiply_exponential_fusion.4) | copy-start | bytes 1540
  158.1 6.0 copy-start.47
  164.1 29.5 %all-to-all-start.2 = ((bf16[8,256,128]{2,1,0:T(8,128)(2,1)}), bf16[8,256,128]{2,1,0:T(8,128)(2,1)S(1)}, u32[]{:S(2)}, u32[]{:S(2)}) async-start(bf16[8,256,128]{2,1,0:T(8,128)(2,1)} %bitcast.13), calls=%async_computation.2 | async-start | bytes 1048576 | tf_op jit(solution)/shard_map/all_to_all | solution.py:234
  167.8 518.7 %reduce-scatter.20.cloned.1.call-start = ((), (), s32[]{:S(2)}) async-start(), calls=%async_computation.26 | async-start | bytes 4325376 | tf_op jit(solution)/shard_map/reduce_scatter | solution.py:276
  168.3 338.3 %copy-start.45 = (f32[1024]{0:T(1024)}, f32[1024]{0:T(1024)S(1)}, u32[]{:S(2)}) copy-start(f32[1024]{0:T(1024)S(1)} %convert_element_type.178) | copy-start | bytes 12292
  197.7 56.3 %copy-start.31 = (bf16[256,1024]{1,0:T(8,128)(2,1)}, bf16[256,1024]{1,0:T(8,128)(2,1)S(1)}, u32[]{:S(2)}) copy-start(bf16[256,1024]{1,0:T(8,128)(2,1)S(1)} %get-tuple-element.178) | copy-start | bytes 1572868
  254.5 4.7 copy-start.1
  254.5 4.6 collective-permute-start.1
  260.6 52.3 %copy-start.33 = (bf16[256,1024]{1,0:T(8,128)(2,1)}, bf16[256,1024]{1,0:T(8,128)(2,1)S(1)}, u32[]{:S(2)}) copy-start(bf16[256,1024]{1,0:T(8,128)(2,1)S(1)} %get-tuple-element.93) | copy-start | bytes 1572868
  388.7 79.1 %copy-start.12 = (bf16[1,256,1024]{2,1,0:T(8,128)(2,1)S(1)}, bf16[1,256,1024]{2,1,0:T(8,128)(2,1)}, u32[]{:S(2)}) copy-start(bf16[1,256,1024]{2,1,0:T(8,128)(2,1)} %param.23) | copy-start | bytes 1572868
  467.8 9.0 copy-start.34
  479.5 283.3 %reduce-scatter.12.cloned.1.call-start = ((), (), s32[]{:S(2)}) async-start(), calls=%async_computation.22 | async-start | bytes 4325376 | tf_op jit(solution)/shard_map/reduce_scatter | solution.py:335
  487.1 6.6 copy-start.13
  487.1 6.6 copy-start.2
  487.1 6.6 copy-start.35
  487.1 6.6 copy-start.37
  495.6 5.5 collective-permute-start.2
  497.2 4.9 copy-start.74
  509.7 7.0 copy-start.32
  511.7 21.0 %all-to-all-start.3 = ((bf16[256,8,128]{2,0,1:T(8,128)(2,1)}), bf16[256,8,128]{2,0,1:T(8,128)(2,1)}, u32[]{:S(2)}, u32[]{:S(2)}) async-start(bf16[256,8,128]{2,0,1:T(8,128)(2,1)} %bitcast.194), calls=%async_computation.3 | async-start | bytes 1048576 | tf_op jit(solution)/shard_map/all_to_all | solution.py:286
  516.6 386.1 %reduce-scatter.14.cloned.1.call-start = ((), (), s32[]{:S(2)}) async-start(), calls=%async_computation.23 | async-start | bytes 4325376 | tf_op jit(solution)/shard_map/reduce_scatter | solution.py:336
  519.4 14.5 copy-start.4
  519.4 14.5 copy-start.86
  519.4 523.1 %reduce-scatter.8.cloned.1.call-start = ((), (), s32[]{:S(2)}) async-start(), calls=%async_computation.20 | async-start | bytes 4325376 | tf_op jit(solution)/shard_map/reduce_scatter | solution.py:333
  534.0 6.5 copy-start.65
  534.0 6.5 copy-start.67
  534.0 6.5 copy-start.69
  534.0 8.0 copy-start.48
  552.0 19.8 %copy-start.8 = (f32[1,255,1024]{2,1,0:T(8,128)S(1)}, f32[1,255,1024]{2,1,0:T(8,128)}, u32[]{:S(2)}) copy-start(f32[1,255,1024]{2,1,0:T(8,128)} %get-tuple-element.103) | copy-start | bytes 3133444
  574.9 607.4 %reduce-scatter.10.cloned.1.call-start = ((), (), s32[]{:S(2)}) async-start(), calls=%async_computation.21 | async-start | bytes 4325376 | tf_op jit(solution)/shard_map/reduce_scatter | solution.py:334
  597.3 766.8 %reduce-scatter.16.cloned.1.call-start = ((), (), s32[]{:S(2)}) async-start(), calls=%async_computation.24 | async-start | bytes 17301504 | tf_op jit(solution)/shard_map/reduce_scatter | solution.py:273
  608.1 943.3 %reduce-scatter.18.cloned.1.call-start = ((), (), s32[]{:S(2)}) async-start(), calls=%async_computation.25 | async-start | bytes 17301504 | tf_op jit(solution)/shard_map/reduce_scatter | solution.py:275
  619.7 4.8 copy-start.57
  619.7 4.8 copy-start.55
  619.7 4.8 copy-start.56
  619.7 5.8 copy-start.43
  619.8 5.7 copy-start.44
  619.8 8.3 copy-start.24
  624.5 5.9 copy-start.22
  624.6 5.8 copy-start.40
  631.4 5.5 collective-permute-start.3
  637.0 48.1 %copy-start.76 = (f32[256]{0:T(256)S(1)}, f32[256]{0:T(256)}, u32[]{:S(2)}) copy-start(f32[256]{0:T(256)} %copy-done.75) | copy-start | bytes 3076
  638.1 46.9 %copy-start.10 = (f32[256,1024]{1,0:T(8,128)S(1)}, f32[256,1024]{1,0:T(8,128)}, u32[]{:S(2)}) copy-start(f32[256,1024]{1,0:T(8,128)} %copy-done.9) | copy-start | bytes 3145732
  (50 other events, 97.6 us)
Sparse Core Ops, SparseCore 0:
  10.9 59.3 all-gather.11
  73.2 57.8 all-gather.9
  133.9 59.5 all-gather.7
  196.3 55.2 all-gather.13
  254.3 55.2 all-gather.15
  312.3 76.3 all-gather.17
  391.6 76.1 all-gather.19
  479.7 142.6 reduce-scatter.19
  625.2 137.6 reduce-scatter.11
  765.5 137.0 reduce-scatter.13
  905.5 136.9 reduce-scatter.7
  1045.2 137.0 reduce-scatter.9
  1185.2 178.8 reduce-scatter.15
  1366.8 184.5 reduce-scatter.17
where the time goes:
time: 1570 us; the launch traced here: 1560 us
  waiting for transfers between devices  1230 us (78%)
  blocking collectives  120 us (8%)
  matrix products  99.1 us (6%)
  other arithmetic  32.3 us (2%)
  local copies, waits for them, and re-layouts  32.1 us (2%)
  starting transfers between devices  29.4 us (2%)
  between operations  16.1 us (1%)
    reduce_scatter x1, waiting for transfers between devices, per_device(): lax.psum_scatter(grad_ffn_value, ('seq', 'rep'), scatter_dimension=0, til...  187 us
    reduce_scatter x1, waiting for transfers between devices, per_device(): lax.psum_scatter(grad_ffn_key, ('seq', 'rep'), scatter_dimension=0, tiled...  182 us
    reduce_scatter x1, waiting for transfers between devices, per_device(): lax.psum_scatter(grad_att_key, ('seq', 'rep'), scatter_dimension=0, tiled...  140 us
    reduce_scatter x1, waiting for transfers between devices, per_device(): lax.psum_scatter(grad_att_value, ('seq', 'rep'), scatter_dimension=0, til...  140 us
    reduce_scatter x1, waiting for transfers between devices, per_device(): lax.psum_scatter(grad_att_output, ('seq', 'rep'), scatter_dimension=0, ti...  140 us
    unnamed x2, blocking collectives  82.7 us
    reduce_scatter x1, waiting for transfers between devices, per_device(): lax.psum_scatter(grad_att_recept, ('seq', 'rep'), scatter_dimension=0, ti...  76.3 us
    all_gather x1, waiting for transfers between devices, per_device(): lax.all_gather(feedforward_lookup_matrix, ('seq', 'rep'), axis=0, tiled=T...  75.8 us
  transfers between devices with their start and end apart: 22, of which 17 were waited for; matrix products, arithmetic and copies ran while one was open for 9% of the time, Pallas kernels for 0%

commit v1 on v0

v1 whole, which is shorter than its diff:
```python
from functools import partial

import jax
import jax.numpy as jnp
from jax import lax
from jax.experimental import pallas as pl
from jax.experimental.pallas import tpu as pltpu
from jax.sharding import Mesh, PartitionSpec as P

EPSILON = 1e-05
F32 = jnp.float32
BF16 = jnp.bfloat16
CHIPS = ("z", "x", "y")
SEQ = ("z", "x")
ALL = ("z", "x", "y", "c")
TILE = 16


def ring(count, step=1):
    return [(i, (i + step) % count) for i in range(count)]


def swap(block):
    return lax.ppermute(block, "c", ring(2))


def along_seq(block, step):
    count = lax.axis_size(SEQ)
    pairs = [(i, i + step) for i in range(count) if 0 <= i + step < count]
    return lax.ppermute(block, SEQ, pairs)


def gather(shard, order):
    have = []
    block = shard
    for axis in order:
        count = lax.axis_size(axis)
        me = lax.axis_index(axis)
        place = sum(1 for other in have if CHIPS.index(other) < CHIPS.index(axis))
        have.append(axis)
        whole = jnp.zeros(block.shape[:place] + (count,) + block.shape[place:], block.dtype)
        piece = block
        for step in range(count):
            if step:
                piece = lax.ppermute(piece, axis, ring(count))
            whole = lax.dynamic_update_index_in_dim(whole, piece, lax.rem(me - step + count, count), place)
        block = whole
    return block.reshape(-1, shard.shape[-1])


def scatter_sum(whole, order):
    columns = whole.shape[-1]
    left = list(CHIPS)
    block = whole.reshape(tuple(lax.axis_size(axis) for axis in CHIPS) + (-1, columns))
    for axis in order:
        count = lax.axis_size(axis)
        me = lax.axis_index(axis)
        place = left.index(axis)
        left.remove(axis)

        def part(step):
            return lax.dynamic_index_in_dim(
                block, lax.rem(me - step + count, count), place, keepdims=False
            )

        total = part(1)
        for step in range(2, count + 1):
            moved = lax.ppermute(total.astype(BF16), axis, ring(count))
            total = moved.astype(F32) + part(step).astype(F32)
        block = total
    return block


def dot(left, right):
    return jnp.dot(left, right, preferred_element_type=F32)


def dot_back(grad, weight):
    return lax.dot_general(grad, weight, (((1,), (1,)), ((), ())), preferred_element_type=F32)


def outer(left, right):
    return lax.dot_general(left, right, (((0,), (0,)), ((), ())), preferred_element_type=F32)


def norm_parts(rows):
    center = jnp.mean(rows, axis=-1, keepdims=True)
    deviation = rows - center
    variance = jnp.mean(deviation * deviation, axis=-1, keepdims=True)
    inverse = lax.rsqrt(variance + EPSILON)
    return deviation * inverse, inverse


def norm_back(grad, zhat, inverse, gain):
    scaled = grad * gain
    return inverse * (
        scaled
        - jnp.mean(scaled, axis=-1, keepdims=True)
        - zhat * jnp.mean(scaled * zhat, axis=-1, keepdims=True)
    )


def shift_down(rows, first):
    return jnp.concatenate([first, rows[:, :-1]], axis=1)


def shift_up(rows, last):
    return jnp.concatenate([rows[:, 1:], last], axis=1)


def shift_rows(rows, distance):
    return pltpu.roll(rows, distance % rows.shape[0], 0)


def fade_tables(rate, reverse):
    breadth = rate.shape[-1]
    place = lax.broadcasted_iota(jnp.int32, (TILE, breadth), 0)
    if reverse:
        place = TILE - 1 - place
    steps = []
    distance = 1
    while distance < TILE:
        factor = jnp.where(place >= distance, jnp.exp(-rate * float(distance)), 0.0)
        steps.append((distance, factor))
        distance *= 2
    passed = jnp.exp(-rate * place.astype(F32))
    before = (place >= 1).astype(F32)
    return steps, passed, before


def scan_tile(terms, steps, reverse):
    for distance, factor in steps:
        terms = terms + factor * shift_rows(terms, -distance if reverse else distance)
    return terms


def wkv_kernel(
    groups, key_ref, value_ref, recept_ref, rate_ref, bonus_ref, num_ref, den_ref,
    gated_ref, prior_num_ref, prior_den_ref,
):
    rows = key_ref.shape[0] // groups
    rate = rate_ref[...]
    bonus = bonus_ref[...]
    steps, passed, before = fade_tables(rate, False)
    tile_fade = jnp.exp(-rate * float(TILE))

    def body(index, carry):
        states = []
        for group in range(groups):
            num, den = carry[2 * group], carry[2 * group + 1]
            at = pl.ds(pl.multiple_of(group * rows + index * TILE, TILE), TILE)
            grown = jnp.exp(key_ref[at, :].astype(F32))
            product = grown * value_ref[at, :].astype(F32)
            inner_num = scan_tile(product, steps, False)
            inner_den = scan_tile(grown, steps, False)
            prior_num = shift_rows(inner_num, 1) * before + passed * num
            prior_den = shift_rows(inner_den, 1) * before + passed * den
            prior_num_ref[at, :] = prior_num
            prior_den_ref[at, :] = prior_den
            wkv = (prior_num + bonus * product) / (prior_den + bonus * grown)
            gated_ref[at, :] = (recept_ref[at, :] * wkv.astype(BF16).astype(F32)).astype(BF16)
            states.append(inner_num[TILE - 1 :, :] + tile_fade * num)
            states.append(inner_den[TILE - 1 :, :] + tile_fade * den)
        return tuple(states)

    start = []
    for group in range(groups):
        start += [num_ref[group : group + 1, :], den_ref[group : group + 1, :]]
    lax.fori_loop(0, rows // TILE, body, tuple(start))


def wkv_back_kernel(
    groups, key_ref, value_ref, prior_num_ref, prior_den_ref, weighted_ref, rate_ref, bonus_ref,
    num_ref, den_ref, dkey_ref, dvalue_ref, decay_ref, first_ref,
):
    rows = key_ref.shape[0] // groups
    rate = rate_ref[...]
    bonus = bonus_ref[...]
    steps, passed, before = fade_tables(rate, True)
    tile_fade = jnp.exp(-rate * float(TILE))
    decay_ref[...] = jnp.zeros_like(decay_ref)
    first_ref[...] = jnp.zeros_like(first_ref)

    def body(step, carry):
        index = rows // TILE - 1 - step
        states = []
        for group in range(groups):
            num, den = carry[2 * group], carry[2 * group + 1]
            at = pl.ds(pl.multiple_of(group * rows + index * TILE, TILE), TILE)
            grown = jnp.exp(key_ref[at, :].astype(F32))
            value = value_ref[at, :].astype(F32)
            prior_num = prior_num_ref[at, :]
            prior_den = prior_den_ref[at, :]
            wkv_den = prior_den + bonus * grown
            wkv = (prior_num + bonus * grown * value) / wkv_den
            grad = weighted_ref[at, :].astype(F32) / wkv_den
            inner_num = scan_tile(grad, steps, True)
            inner_den = scan_tile(-grad * wkv, steps, True)
            lam_num = shift_rows(inner_num, -1) * before + passed * num
            lam_den = shift_rows(inner_den, -1) * before + passed * den
            bonus_grad = bonus * grad
            dvalue_ref[at, :] = (grown * (bonus_grad + lam_num)).astype(BF16)
            direct = bonus_grad * (value - wkv)
            dkey_ref[at, :] = (grown * (direct + lam_num * value + lam_den)).astype(BF16)
            first_ref[...] += grown * direct
            decay_ref[...] += lam_num * prior_num + lam_den * prior_den
            states.append(inner_num[:1, :] + tile_fade * num)
            states.append(inner_den[:1, :] + tile_fade * den)
        return tuple(states)

    start = []
    for group in range(groups):
        start += [num_ref[group : group + 1, :], den_ref[group : group + 1, :]]
    lax.fori_loop(0, rows // TILE, body, tuple(start))


def wkv_call(kernel, groups, shapes, operands):
    return pl.pallas_call(
        partial(kernel, groups),
        out_shape=shapes,
        compiler_params=pltpu.CompilerParams(vmem_limit_bytes=32 << 20),
    )(*operands)


def per_device(
    layer_incoming,
    series_extents,
    emitted_adjoint,
    norm1_scaling,
    norm1_offset,
    mixer_lookup_portion,
    mixer_payload_portion,
    mixer_accept_portion,
    temporal_fading_log,
    present_step_reward,
    mixer_lookup_matrix,
    mixer_payload_matrix,
    mixer_accept_matrix,
    mixer_emit_matrix,
    norm2_scaling,
    norm2_offset,
    feedforward_lookup_portion,
    feedforward_accept_portion,
    feedforward_lookup_matrix,
    feedforward_payload_matrix,
    feedforward_accept_matrix,
):
    devices = lax.axis_size(ALL)
    chips = lax.axis_size(CHIPS)
    parts = lax.axis_size(SEQ)
    core = lax.axis_index("c")
    place = lax.axis_index(SEQ)
    rows, breadth = layer_incoming.shape[1:]
    own_rows = mixer_lookup_matrix.shape[0]
    hidden_rows = feedforward_payload_matrix.shape[0]

    vectors = jnp.stack(
        [
            norm1_scaling, norm1_offset, mixer_lookup_portion, mixer_payload_portion,
            mixer_accept_portion, norm2_scaling, norm2_offset, feedforward_lookup_portion,
            feedforward_accept_portion, temporal_fading_log, present_step_reward,
        ]
    )
    vectors = lax.all_to_all(
        jnp.broadcast_to(vectors[None], (devices,) + vectors.shape), ALL, 0, 0, tiled=True
    )
    vectors = vectors.astype(F32).transpose(1, 0, 2)
    gain1, bias1, mix_k, mix_v, mix_r, gain2, bias2, mix_fk, mix_fr = vectors[:9].reshape(9, breadth)
    channel = lax.dynamic_index_in_dim(
        vectors[9:].reshape(2, chips, 2, own_rows), core, 2, keepdims=False
    ).reshape(2, 1, -1)
    rate, bonus = jnp.exp(channel[0]), jnp.exp(channel[1])

    def by_core(matrix, width):
        return matrix.reshape(own_rows, -1, 2, width).swapaxes(0, 2)

    halves = jnp.concatenate(
        [
            by_core(matrix, width).swapaxes(1, 2).reshape(2, own_rows, -1)
            for matrix, width in (
                (mixer_lookup_matrix, own_rows),
                (mixer_payload_matrix, own_rows),
                (mixer_accept_matrix, own_rows),
                (feedforward_lookup_matrix, hidden_rows),
                (feedforward_accept_matrix, breadth // 2),
            )
        ],
        axis=-1,
    )
    mine = lax.dynamic_index_in_dim(halves, core, 0, keepdims=False)
    other = swap(lax.dynamic_index_in_dim(halves, 1 - core, 0, keepdims=False))
    both = lambda own, other: jnp.where(core == 0, jnp.stack([own, other]), jnp.stack([other, own]))
    mine_of = lambda pair: lax.dynamic_index_in_dim(pair, core, 0, keepdims=False)
    other_of = lambda pair: lax.dynamic_index_in_dim(pair, 1 - core, 0, keepdims=False)
    pair = both(mine, other).reshape(2 * own_rows, -1)
    half = breadth // 2
    hidden = pair.shape[1] - 4 * half
    weights_att = gather(pair[:, : 3 * half], ("z", "x", "y"))
    weight_o = gather(mixer_emit_matrix, ("z", "y", "x"))
    weight_fr = gather(pair[:, 3 * half + hidden :], ("z", "y", "x"))
    weight_fk = gather(pair[:, 3 * half : 3 * half + hidden], ("x", "z", "y"))
    weight_fv = gather(feedforward_payload_matrix, ("y", "z", "x"))
    weight_k, weight_v, weight_r = (weights_att[:, i * half : (i + 1) * half] for i in range(3))

    begins = jnp.cumsum(series_extents[0]) - series_extents[0]
    starts = jnp.any(jnp.arange(parts)[:, None] * rows == begins[None, :], axis=1)
    joined = jnp.where(starts, 0.0, 1.0).astype(F32)
    joined = both(joined, swap(joined))
    keep = lax.dynamic_index_in_dim(joined, place, 1)[:, :, None]
    after = jnp.concatenate([joined[:, 1:], jnp.zeros((2, 1), F32)], axis=1)
    keep_after = lax.dynamic_index_in_dim(after, place, 1)[:, :, None]
    index = jnp.arange(parts)
    began = jnp.where((joined == 0.0) & (index[None] <= place), index[None], -1).max(axis=1)
    reach = ((index[None] < place) & (index[None] >= began[:, None])).astype(F32)
    begun = jnp.where((joined == 0.0) & (index[None] > place), index[None], parts).min(axis=1)
    reach_back = ((index[None] > place) & (index[None] < begun[:, None])).astype(F32)

    def entering(ends, reached, distance):
        fades = jnp.exp(-rate[None] * (float(rows) * jnp.maximum(distance, 0).astype(F32))[:, None, None])
        return jnp.sum(ends * (reached.T[:, None, :, None] * fades[:, :, None]), axis=0)

    def spread(ends):
        return lax.all_to_all(
            jnp.broadcast_to(ends[None], (parts,) + ends.shape), SEQ, 0, 0, tiled=True
        )

    own_in = jnp.concatenate([layer_incoming, emitted_adjoint], axis=0)
    both_in = both(own_in, swap(own_in))
    inputs = both_in[:, 0].astype(F32)
    cotangent = both_in[:, 1].astype(F32)
    behind = along_seq(both_in[:, 0, rows - 1 :], 1).astype(F32)
    flat = lambda element: element.reshape(2 * rows, -1)

    zhat1, inverse1 = norm_parts(inputs)
    normed = zhat1 * gain1 + bias1
    normed_behind = (norm_parts(behind)[0] * gain1 + bias1) * keep
    step1 = normed - shift_down(normed, normed_behind)
    mixed = lambda value, step, share: flat(value - step * (1.0 - share)).astype(BF16)
    mixed_k, mixed_v, mixed_r = (mixed(normed, step1, share) for share in (mix_k, mix_v, mix_r))
    keys = dot(mixed_k, weight_k).astype(BF16)
    values = dot(mixed_v, weight_v).astype(BF16)
    recept = jax.nn.sigmoid(dot(mixed_r, weight_r))

    token = jnp.arange(rows, dtype=F32)[:, None]
    grown = jnp.exp(keys.astype(F32)).reshape(2, rows, half)
    product = grown * values.astype(F32).reshape(2, rows, half)
    to_end = jnp.exp(-rate * (rows - 1.0 - token))[None]
    ends = jnp.stack([(product * to_end).sum(axis=1), (grown * to_end).sum(axis=1)])
    enter = entering(spread(ends), reach, place - 1 - index)
    shape = lambda kind: jax.ShapeDtypeStruct((2 * rows, half), kind)
    gated, prior_num, prior_den = wkv_call(
        wkv_kernel, 2, (shape(BF16), shape(F32), shape(F32)),
        (keys, values, recept, rate, bonus, enter[0], enter[1]),
    )

    attended = dot(gated, weight_o)
    middle = inputs + (attended + swap(attended)).reshape(2, rows, breadth)
    zhat2, inverse2 = norm_parts(middle)
    normed2 = zhat2 * gain2 + bias2
    step2 = normed2 - shift_down(normed2, along_seq(normed2[:, rows - 1 :], 1) * keep)
    ffn_k, ffn_r = (mixed(normed2, step2, share) for share in (mix_fk, mix_fr))
    pre_hidden = jax.nn.relu(dot(ffn_k, weight_fk))
    hidden_act = jnp.square(pre_hidden).astype(BF16)
    gate_half = jax.nn.sigmoid(dot(ffn_r, weight_fr))
    gate_other = swap(gate_half)
    gate = jnp.concatenate(
        [jnp.where(core == 0, gate_half, gate_other), jnp.where(core == 0, gate_other, gate_half)], axis=1
    )
    value_part = dot(hidden_act, weight_fv)
    value_out = value_part + swap(value_part)
    block_output = mine_of(
        (middle + (gate * value_out).reshape(2, rows, breadth)).astype(BF16)
    )

    d_value_out = (flat(cotangent) * gate).astype(BF16)
    d_gate_pre = flat(cotangent) * value_out * gate * (1.0 - gate)
    d_gate_pre = lax.dynamic_slice_in_dim(d_gate_pre, core * half, half, 1).astype(BF16)
    d_hidden = dot_back(d_value_out, weight_fv)
    d_pre_hidden = (d_hidden * 2.0 * pre_hidden).astype(BF16)
    grad_fv = outer(hidden_act, d_value_out).astype(BF16)
    grad_fk = outer(ffn_k, d_pre_hidden).astype(BF16)
    grad_fr = outer(ffn_r, d_gate_pre).astype(BF16)
    back = lambda grad, weight: dot_back(grad, weight).reshape(2, rows, breadth)

    def mix_back(grads, shares, step):
        share_grads = [jnp.sum(grad * step, axis=(0, 1)) for grad in grads]
        direct = sum(grad * share for grad, share in zip(grads, shares))
        shifted = sum(grad * (1.0 - share) for grad, share in zip(grads, shares))
        return share_grads, direct, shifted

    grads2 = (back(d_pre_hidden, weight_fk), back(d_gate_pre, weight_fr))
    (share_fk, share_fr), direct2, shifted2 = mix_back(grads2, (mix_fk, mix_fr), step2)
    returned2 = along_seq(shifted2[:, :1] * keep, -1)
    part2 = direct2 + shift_up(shifted2, returned2)
    d_normed2 = part2 + swap(part2)
    d_middle = cotangent + norm_back(d_normed2, zhat2, inverse2, gain2)
    grad_gain2 = jnp.sum(mine_of(d_normed2 * zhat2), axis=0)
    grad_bias2 = jnp.sum(mine_of(d_normed2), axis=0)

    d_attended = flat(d_middle).astype(BF16)
    grad_o = outer(gated, d_attended).astype(BF16)
    d_gated = dot_back(d_attended, weight_o)
    d_weighted = (d_gated * recept).astype(BF16)
    wkv_den = prior_den + bonus * flat(grown)
    wkv = (prior_num + bonus * flat(product)) / wkv_den
    d_recept_pre = (
        d_gated * wkv.astype(BF16).astype(F32) * recept * (1.0 - recept)
    ).astype(BF16)
    from_begin = jnp.exp(-rate * token)[None]
    per_den = d_weighted.astype(F32) / wkv_den
    begin_num = (per_den.reshape(2, rows, half) * from_begin).sum(axis=1)
    begin_den = -((per_den * wkv).reshape(2, rows, half) * from_begin).sum(axis=1)
    enter_back = entering(spread(jnp.stack([begin_num, begin_den])), reach_back, index - place - 1)
    small = jax.ShapeDtypeStruct((TILE, half), F32)
    d_keys, d_values, decay_sum, first_sum = wkv_call(
        wkv_back_kernel, 2, (shape(BF16), shape(BF16), small, small),
        (keys, values, prior_num, prior_den, d_weighted, rate, bonus, enter_back[0], enter_back[1]),
    )
    grad_decay = -rate[0] * jnp.exp(-rate[0]) * decay_sum.sum(axis=0)
    grad_first = first_sum.sum(axis=0)

    grad_att = jnp.concatenate(
        [outer(mixed_k, d_keys), outer(mixed_v, d_values), outer(mixed_r, d_recept_pre)], axis=1
    ).astype(BF16)
    grads1 = (back(d_keys, weight_k), back(d_values, weight_v), back(d_recept_pre, weight_r))
    (share_k, share_v, share_r), direct1, shifted1 = mix_back(grads1, (mix_k, mix_v, mix_r), step1)
    returned1 = along_seq(shifted1[:, :1] * keep, -1)
    part1 = direct1 + shift_up(shifted1, returned1)
    d_normed = mine_of(part1) + swap(other_of(part1))
    own_zhat = mine_of(zhat1)
    input_grad = mine_of(d_middle) + norm_back(d_normed, own_zhat, mine_of(inverse1), gain1)
    grad_gain1 = jnp.sum(d_normed * own_zhat, axis=0)
    grad_bias1 = jnp.sum(d_normed, axis=0)

    def by_channel(grad):
        whole = jnp.zeros((chips, 2, own_rows), F32)
        return lax.dynamic_update_index_in_dim(
            whole, grad.reshape(chips, own_rows), core, 1
        ).reshape(breadth)

    grads = jnp.stack(
        [
            grad_gain1, grad_bias1, share_k, share_v, share_r, by_channel(grad_decay),
            by_channel(grad_first), grad_gain2, grad_bias2, share_fk, share_fr,
        ]
    )
    grads = grads.reshape(11, devices, own_rows).swapaxes(0, 1)
    grads = lax.all_to_all(grads, ALL, 0, 0, tiled=True).sum(axis=0)

    sum_fv = scatter_sum(grad_fv, ("x", "z", "y"))
    sum_fk = scatter_sum(grad_fk, ("y", "z", "x"))
    sum_fr = scatter_sum(grad_fr, ("x", "y", "z"))
    sum_o = scatter_sum(grad_o, ("x", "y", "z"))
    sum_att = scatter_sum(grad_att, ("y", "x", "z"))

    sums = jnp.concatenate([sum_att, sum_fk, sum_fr], axis=1).reshape(2, own_rows, -1)
    mine = lax.dynamic_index_in_dim(sums, core, 0, keepdims=False)
    other = swap(lax.dynamic_index_in_dim(sums, 1 - core, 0, keepdims=False))
    low, high = jnp.where(core == 0, mine, other), jnp.where(core == 0, other, mine)

    def columns(start, size, width):
        pieces = [piece[:, start : start + size].reshape(own_rows, -1, 1, width) for piece in (low, high)]
        return jnp.concatenate(pieces, axis=2).reshape(own_rows, 2 * size)

    return (
        block_output[None],
        input_grad[None],
        *(grads[i] for i in range(7)),
        columns(0, half, own_rows),
        columns(half, half, own_rows),
        columns(2 * half, half, own_rows),
        sum_o,
        *(grads[i] for i in range(7, 11)),
        columns(3 * half, hidden, hidden_rows),
        sum_fv,
        columns(3 * half + hidden, half, half),
    )


def solution(mesh):
    parts, groups = mesh.shape["seq"], mesh.shape["rep"]
    width = groups // 2
    fine = Mesh(mesh.devices.reshape(parts // width, width, width, 2), ALL)
    tokens = P(("y", "c"), SEQ, None)
    vector = P(ALL)
    matrix = P(ALL, None)
    return jax.shard_map(
        per_device,
        mesh=fine,
        in_specs=(
            (tokens, P(("y", "c"), None), tokens)
            + (vector,) * 7
            + (matrix,) * 4
            + (vector,) * 4
            + (matrix,) * 3
        ),
        out_specs=(
            (tokens, tokens) + (vector,) * 7 + (matrix,) * 4 + (vector,) * 4 + (matrix,) * 3
        ),
        check_vma=False,
    )
```

time: 1570 us -> 564 us (0.36)
  waiting for transfers between devices: 1230 us -> 268 us
  blocking collectives: 120 us -> 0 us
  matrix products: 99.1 us -> 37.1 us
  local copies, waits for them, and re-layouts: 32.1 us -> 93.8 us
  starting transfers between devices: 29.4 us -> 84.7 us
  other arithmetic: 32.3 us -> 63.8 us
    reduce_scatter x7 -> x0, waiting for transfers between devices: 865 us -> none  [the longest x1 187 us: per_device(): lax.psum_scatter(grad_ffn_value, ('seq', 'rep'), scatter_dimension=0, til...]
    all_gather x7 -> x0, waiting for transfers between devices: 324 us -> none  [the longest x1 75.8 us: per_device(): lax.all_gather(feedforward_lookup_matrix, ('seq', 'rep'), axis=0, tiled=T...]
    ppermute x4 -> x63, waiting for transfers between devices: 7.92 us -> 243 us  [the longest x25 153 us: scatter_sum(): moved = lax.ppermute(total.astype(BF16), axis, ring(count))]
    unnamed x2 -> x0, blocking collectives: 82.7 us -> none
    dot_general x27 -> x21, matrix products: 99.1 us -> 37.1 us  [the longest x7 14.1 us: dot_back(): lax.dot_general(grad, weight, (((1,), (1,)), ((), ())), preferred_element...]
    ppermute x4 -> x63, starting transfers between devices: 10.1 us -> 59.6 us  [the longest x25 32.4 us: scatter_sum(): moved = lax.ppermute(total.astype(BF16), axis, ring(count))]
    all_to_all x2 -> x0, blocking collectives: 37.7 us -> none  [the longest x1 19.6 us: per_device(): lax.all_to_all(feature_lookup_derivative.astype(jnp.bfloat16), 'seq', spl...]
    dynamic_update_slice x0 -> x42, local copies, waits for them, and re-layouts: none -> 32.6 us  [the longest x40 32.5 us: gather(): lax.dynamic_update_index_in_dim(whole, piece, lax.rem(me - step + count,...]
  transfers between devices with their start and end apart: 22 -> 67, of which waited for: 17 -> 29; matrix products, arithmetic and copies ran while one was open for 9% -> 29% of each run, Pallas kernels for 0% -> 1%
where the time goes in v1:
time: 564 us; the launch traced here: 556 us
  waiting for transfers between devices  268 us (48%)
  local copies, waits for them, and re-layouts  93.8 us (17%)
  starting transfers between devices  84.7 us (15%)
  other arithmetic  63.8 us (11%)
  matrix products  37.1 us (7%)
    ppermute x25, waiting for transfers between devices, scatter_sum(): moved = lax.ppermute(total.astype(BF16), axis, ring(count))  153 us
    ppermute x25, waiting for transfers between devices, gather(): piece = lax.ppermute(piece, axis, ring(count))  89.2 us
    dynamic_update_slice x40, local copies, waits for them, and re-layouts, gather(): lax.dynamic_update_index_in_dim(whole, piece, lax.rem(me - step + count,...  32.5 us
    ppermute x25, starting transfers between devices, scatter_sum(): moved = lax.ppermute(total.astype(BF16), axis, ring(count))  32.4 us
    all_to_all x2, waiting for transfers between devices, spread(): lax.all_to_all(jnp.broadcast_to(ends[None], (parts,) + ends.shape), SEQ,...  20.1 us
    unnamed x174, local copies, waits for them, and re-layouts  19.3 us
    ppermute x25, starting transfers between devices, gather(): piece = lax.ppermute(piece, axis, ring(count))  17.6 us
    add x15, other arithmetic, scatter_sum(): total = moved.astype(F32) + part(step).astype(F32)  15.6 us
  transfers between devices with their start and end apart: 67, of which 29 were waited for; matrix products, arithmetic and copies ran while one was open for 29% of the time, Pallas kernels for 1%

profile of v1, /device:TPU:0, one launch (start us, length us, event | category | flops | bytes accessed | tf_op | source)
XLA Modules:
  0.0 555.8 jit_solution(17825150545263675576)
XLA Ops:
  3.0 7.3 %all-to-all-start = ((bf16[32,2,176]{2,1,0:T(2,128)(2,1)}), bf16[32,2,176]{2,1,0:T(2,128)(2,1)S(1)}, u32[]{:S(2)}, u32[]{:S(2)}) async-start(bf16[32,2,176]{2,1,0:T(2,128)(2,1)} %reshape.895), calls=%async_computation | async-start | bytes 65536 | tf_op jit(solution)/shard_map/all_to_all | solution.py:264
  27.2 4.6 collective-permute-done.10
  31.8 6.0 %collective-permute-done.11 = bf16[32,1024]{1,0:T(8,128)(2,1)S(1)} collective-permute-done((bf16[32,1024]{1,0:T(8,128)(2,1)S(1)}, bf16[32,1024]{1,0:T(8,128)(2,1)S(1)}, u32[]{:S(2)}, u32[]{:S(2)}) %collective-permute-start.11) | collective-permute-done | bytes 65568 | tf_op jit(solution)/shard_map/ppermute | solution.py:45
  43.3 6.5 %collective-permute-done.16 = bf16[64,512]{1,0:T(8,128)(2,1)S(1)} collective-permute-done((bf16[64,512]{1,0:T(8,128)(2,1)S(1)}, bf16[64,512]{1,0:T(8,128)(2,1)S(1)}, u32[]{:S(2)}, u32[]{:S(2)}) %collective-permute-start.16) | collective-permute-done | bytes 65568 | tf_op jit(solution)/shard_map/ppermute | solution.py:45
  49.8 8.8 %collective-permute-done.17 = bf16[64,512]{1,0:T(8,128)(2,1)S(1)} collective-permute-done((bf16[64,512]{1,0:T(8,128)(2,1)S(1)}, bf16[64,512]{1,0:T(8,128)(2,1)S(1)}, u32[]{:S(2)}, u32[]{:S(2)}) %collective-permute-start.17) | collective-permute-done | bytes 65568 | tf_op jit(solution)/shard_map/ppermute | solution.py:45
  60.2 6.0 %collective-permute-done.18 = bf16[64,512]{1,0:T(8,128)(2,1)S(1)} collective-permute-done((bf16[64,512]{1,0:T(8,128)(2,1)S(1)}, bf16[64,512]{1,0:T(8,128)(2,1)S(1)}, u32[]{:S(2)}, u32[]{:S(2)}) %collective-permute-start.18) | collective-permute-done | bytes 65568 | tf_op jit(solution)/shard_map/ppermute | solution.py:45
  72.7 7.1 %collective-permute-done.5 = bf16[64,1536]{1,0:T(8,128)(2,1)S(1)} collective-permute-done((bf16[64,1536]{1,0:T(8,128)(2,1)S(1)}, bf16[64,1536]{1,0:T(8,128)(2,1)S(1)}, u32[]{:S(2)}, u32[]{:S(2)}) %collective-permute-start.5) | collective-permute-done | bytes 196640 | tf_op jit(solution)/shard_map/ppermute | solution.py:45
  85.2 10.9 %collective-permute-done.6 = bf16[64,1536]{1,0:T(8,128)(2,1)S(1)} collective-permute-done((bf16[64,1536]{1,0:T(8,128)(2,1)S(1)}, bf16[64,1536]{1,0:T(8,128)(2,1)S(1)}, u32[]{:S(2)}, u32[]{:S(2)}) %collective-permute-start.6) | collective-permute-done | bytes 196640 | tf_op jit(solution)/shard_map/ppermute | solution.py:45
  103.4 2.5 collective-permute-start.1
  108.6 2.3 bitcast_dynamic-update-slice_fusion.16
  122.0 1.9 bitcast_dynamic-update-slice_fusion.11
  125.5 2.3 collective-permute-start.25
  129.7 6.7 %collective-permute-done.30 = bf16[2,128,1024]{2,1,0:T(8,128)(2,1)S(1)} collective-permute-done((bf16[2,128,1024]{2,1,0:T(8,128)(2,1)}, bf16[2,128,1024]{2,1,0:T(8,128)(2,1)S(1)}, u32[]{:S(2)}, u32[]{:S(2)}) %collective-permute-start.30) | collective-permute-done | bytes 524320 | tf_op jit(solution)/shard_map/ppermute | solution.py:45
  143.2 8.7 %all-to-all-start.1 = ((f32[8,2,2,512]{3,2,1,0:T(2,128)}), f32[8,2,2,512]{3,2,1,0:T(2,128)S(1)}, u32[]{:S(2)}, u32[]{:S(2)}) async-start(f32[8,2,2,512]{3,2,1,0:T(2,128)} %broadcast_in_dim.289), calls=%async_computation.1 | async-start | bytes 131072 | tf_op jit(solution)/shard_map/all_to_all | solution.py:323
  151.9 2.4 fusion.22.recept_ref
  154.3 20.1 %all-to-all-done.1 = f32[8,2,2,512]{3,2,1,0:T(2,128)S(1)} async-done(((f32[8,2,2,512]{3,2,1,0:T(2,128)}), f32[8,2,2,512]{3,2,1,0:T(2,128)S(1)}, u32[]{:S(2)}, u32[]{:S(2)}) %all-to-all-start.1) | async-done | bytes 65568 | tf_op jit(solution)/shard_map/all_to_all | solution.py:323
  174.5 2.3 shard_map.356
  186.9 3.4 bitcast_dynamic-update-slice_fusion.2
  190.6 2.1 fusion.62
  193.0 2.3 multiply_reduce_fusion.6
  195.3 4.5 multiply_add_fusion.2
  199.8 2.6 collective-permute-start.15
  202.4 29.8 %collective-permute-done.26 = bf16[4,2,64,2048]{3,2,1,0:T(8,128)(2,1)} collective-permute-done((bf16[4,2,64,2048]{3,2,1,0:T(8,128)(2,1)}, bf16[4,2,64,2048]{3,2,1,0:T(8,128)(2,1)}, u32[]{:S(2)}, u32[]{:S(2)}) %collective-permute-start.26) | collective-permute-done | bytes 2097184 | tf_op jit(solution)/shard_map/ppermute | solution.py:45
  238.6 2.4 fusion.97
  240.9 2.4 fusion.49
  244.6 4.6 multiply_convert_fusion
  249.2 2.4 convolution_convert_fusion.1
  255.0 4.8 convolution_convert_fusion
  262.8 2.4 fusion.98
  265.2 2.2 fusion.16
  272.2 2.4 multiply_reduce_fusion
  277.6 2.6 fusion.28
  280.2 41.2 %collective-permute-done.47 = bf16[4,2,64,512]{3,2,0,1:T(8,128)(2,1)} collective-permute-done((bf16[4,2,64,512]{3,2,0,1:T(8,128)(2,1)}, bf16[4,2,64,512]{3,2,0,1:T(8,128)(2,1)}, u32[]{:S(2)}, u32[]{:S(2)}) %collective-permute-start.47) | collective-permute-done | bytes 524320 | tf_op jit(solution)/shard_map/ppermute | solution.py:68
  324.2 2.5 maximum_add_fusion
  326.8 2.9 collective-permute-done.48
  330.2 2.6 convert_add_fusion.1
  332.8 2.5 collective-permute-start.43
  336.7 2.5 convert_add_fusion
  340.3 9.2 %collective-permute-done.43 = bf16[2,64,2048]{2,1,0:T(8,128)(2,1)S(1)} collective-permute-done((bf16[2,64,2048]{2,1,0:T(8,128)(2,1)S(1)}, bf16[2,64,2048]{2,1,0:T(8,128)(2,1)S(1)}, u32[]{:S(2)}, u32[]{:S(2)}) %collective-permute-start.43) | collective-permute-done | bytes 524320 | tf_op jit(solution)/shard_map/ppermute | solution.py:68
  351.7 10.5 %collective-permute-done.59 = bf16[2,128,1024]{2,1,0:T(8,128)(2,1)S(1)} collective-permute-done((bf16[2,128,1024]{2,1,0:T(8,128)(2,1)S(1)}, bf16[2,128,1024]{2,1,0:T(8,128)(2,1)S(1)}, u32[]{:S(2)}, u32[]{:S(2)}) %collective-permute-start.59) | collective-permute-done | bytes 524320 | tf_op jit(solution)/shard_map/ppermute | solution.py:68
  363.1 11.7 %collective-permute-done.51 = bf16[64,512]{1,0:T(8,128)(2,1)S(1)} collective-permute-done((bf16[64,512]{1,0:T(8,128)(2,1)S(1)}, bf16[64,512]{1,0:T(8,128)(2,1)S(1)}, u32[]{:S(2)}, u32[]{:S(2)}) %collective-permute-start.51) | collective-permute-done | bytes 65568 | tf_op jit(solution)/shard_map/ppermute | solution.py:68
  376.5 9.6 %collective-permute-done.60 = bf16[2,128,1024]{2,1,0:T(8,128)(2,1)S(1)} collective-permute-done((bf16[2,128,1024]{2,1,0:T(8,128)(2,1)S(1)}, bf16[2,128,1024]{2,1,0:T(8,128)(2,1)S(1)}, u32[]{:S(2)}, u32[]{:S(2)}) %collective-permute-start.60) | collective-permute-done | bytes 524320 | tf_op jit(solution)/shard_map/ppermute | solution.py:68
  390.1 1.9 fusion.88
  393.7 2.4 fusion.87
  397.1 5.8 %all-to-all-start.2 = ((f32[8,2,2,512]{3,2,1,0:T(2,128)}), f32[8,2,2,512]{3,2,1,0:T(2,128)S(1)}, u32[]{:S(2)}, u32[]{:S(2)}) async-start(f32[8,2,2,512]{3,2,1,0:T(2,128)} %broadcast_in_dim.335), calls=%async_computation.2 | async-start | bytes 131072 | tf_op jit(solution)/shard_map/all_to_all | solution.py:323
  403.0 2.2 constant_dynamic-slice_fusion.1
  406.1 2.0 collective-permute-start.53
  412.0 2.9 shard_map.357
  431.0 3.9 maximum_add_fusion.1
  436.6 2.7 collective-permute-start.46
  442.8 24.3 %collective-permute-done.54 = bf16[4,32,1024]{2,1,0:T(8,128)(2,1)S(1)} collective-permute-done((bf16[4,32,1024]{2,1,0:T(8,128)(2,1)S(1)}, bf16[4,32,1024]{2,1,0:T(8,128)(2,1)S(1)}, u32[]{:S(2)}, u32[]{:S(2)}) %collective-permute-start.54) | collective-permute-done | bytes 262176 | tf_op jit(solution)/shard_map/ppermute | solution.py:68
  467.3 4.3 collective-permute-start.55
  473.5 2.4 collective-permute-start.56
  476.8 2.9 collective-permute-done.56
  481.4 4.6 collective-permute-done.57
  487.4 2.3 convert_add_fusion.2
  489.8 4.3 collective-permute-start.38
  494.2 9.9 %collective-permute-done.38 = bf16[4,64,1536]{2,1,0:T(8,128)(2,1)S(1)} collective-permute-done((bf16[4,64,1536]{2,1,0:T(8,128)(2,1)S(1)}, bf16[4,64,1536]{2,1,0:T(8,128)(2,1)S(1)}, u32[]{:S(2)}, u32[]{:S(2)}) %collective-permute-start.38) | collective-permute-done | bytes 786464 | tf_op jit(solution)/shard_map/ppermute | solution.py:68
  504.5 9.4 %collective-permute-done.39 = bf16[64,1536]{1,0:T(8,128)(2,1)S(1)} collective-permute-done((bf16[64,1536]{1,0:T(8,128)(2,1)S(1)}, bf16[64,1536]{1,0:T(8,128)(2,1)S(1)}, u32[]{:S(2)}, u32[]{:S(2)}) %collective-permute-start.39) | collective-permute-done | bytes 196640 | tf_op jit(solution)/shard_map/ppermute | solution.py:68
  514.1 7.4 %collective-permute-done.40 = bf16[64,1536]{1,0:T(8,128)(2,1)S(1)} collective-permute-done((bf16[64,1536]{1,0:T(8,128)(2,1)S(1)}, bf16[64,1536]{1,0:T(8,128)(2,1)S(1)}, u32[]{:S(2)}, u32[]{:S(2)}) %collective-permute-start.40) | collective-permute-done | bytes 196640 | tf_op jit(solution)/shard_map/ppermute | solution.py:68
  521.7 7.4 %collective-permute-done.41 = bf16[64,1536]{1,0:T(8,128)(2,1)S(1)} collective-permute-done((bf16[64,1536]{1,0:T(8,128)(2,1)S(1)}, bf16[64,1536]{1,0:T(8,128)(2,1)S(1)}, u32[]{:S(2)}, u32[]{:S(2)}) %collective-permute-start.41) | collective-permute-done | bytes 196640 | tf_op jit(solution)/shard_map/ppermute | solution.py:68
  532.0 3.4 all-to-all-start.3
  535.4 2.5 fusion.37
  537.9 4.8 all-to-all-done.3
  (536 shorter events, 165.7 us)
Async XLA Ops:
  3.0 18.3 %all-to-all-start = ((bf16[32,2,176]{2,1,0:T(2,128)(2,1)}), bf16[32,2,176]{2,1,0:T(2,128)(2,1)S(1)}, u32[]{:S(2)}, u32[]{:S(2)}) async-start(bf16[32,2,176]{2,1,0:T(2,128)(2,1)} %reshape.895), calls=%async_computation | async-start | bytes 65536 | tf_op jit(solution)/shard_map/all_to_all | solution.py:264
  12.5 87.3 %collective-permute-start = (bf16[2,256,1024]{2,1,0:T(8,128)(2,1)S(1)}, bf16[2,256,1024]{2,1,0:T(8,128)(2,1)}, u32[]{:S(2)}, u32[]{:S(2)}) collective-permute-start(bf16[2,256,1024]{2,1,0:T(8,128)(2,1)S(1)} %constant_dynamic-update-slice_fusion), channel_id=1, source_target_pairs={{0,1},{1,0},{2,3},{3,2},{4,5},{5,4},{6,7},{7,6},{8,9},{9,8},{10,11... | collective-permute-start | bytes 3145736 | tf_op jit(solution)/shard_map/ppermute | solution.py:24
  13.3 7.0 %collective-permute-start.2 = (f32[8]{0:T(128)S(1)}, f32[8]{0:T(128)S(1)}, u32[]{:S(2)}, u32[]{:S(2)}) collective-permute-start(f32[8]{0:T(128)S(1)} %get-tuple-element.133), channel_id=1, source_target_pairs={{0,1},{1,0},{2,3},{3,2},{4,5},{5,4},{6,7},{7,6},{8,9},{9,8},{10,11... | collective-permute-start | bytes 104 | tf_op jit(solution)/shard_map/ppermute | solution.py:24
  15.6 23.0 %collective-permute-start.3 = (bf16[32,4096]{1,0:T(8,128)(2,1)S(1)}, bf16[32,4096]{1,0:T(8,128)(2,1)S(1)}, u32[]{:S(2)}, u32[]{:S(2)}) collective-permute-start(bf16[32,4096]{1,0:T(8,128)(2,1)S(1)} %get-tuple-element.97), channel_id=1, source_target_pairs={{0,1},{1,0},{2,3},{3,2},{4,5},{5,4},{6,7},{7,6},{8,9},{9,8},{10,11... | collective-permute-start | bytes 786440 | tf_op jit(solution)/shard_map/ppermute | solution.py:24
  15.9 9.8 %collective-permute-start.9 = (bf16[32,1024]{1,0:T(8,128)(2,1)S(1)}, bf16[32,1024]{1,0:T(8,128)(2,1)S(1)}, u32[]{:S(2)}, u32[]{:S(2)}) collective-permute-start(bf16[32,1024]{1,0:T(8,128)(2,1)S(1)} %copy-done.67), channel_id=1, source_target_pairs={{0,8},{8,16},{16,24},{24,0},{1,9},{9,17},{17,25},{25,1},{2,10},{10... | collective-permute-start | bytes 196616 | tf_op jit(solution)/shard_map/ppermute | solution.py:45
  17.6 21.4 %collective-permute-start.27 = (bf16[128,1024]{1,0:T(8,128)(2,1)}, bf16[128,1024]{1,0:T(8,128)(2,1)}, u32[]{:S(2)}, u32[]{:S(2)}) collective-permute-start(bf16[128,1024]{1,0:T(8,128)(2,1)} %param.40), channel_id=1, source_target_pairs={{0,2},{2,0},{1,3},{3,1},{4,6},{6,4},{5,7},{7,5},{8,10},{10,8},{9,1... | collective-permute-start | bytes 786440 | tf_op jit(solution)/shard_map/ppermute | solution.py:45
  37.9 22.2 %collective-permute-start.12 = (bf16[4,32,1024]{2,1,0:T(8,128)(2,1)S(1)}, bf16[4,32,1024]{2,1,0:T(8,128)(2,1)S(1)}, u32[]{:S(2)}, u32[]{:S(2)}) collective-permute-start(bf16[4,32,1024]{2,1,0:T(8,128)(2,1)S(1)} %bitcast_dynamic-update-slice_fusion.37), channel_id=1, source_target_pairs={{0,2},{2,0},{1,3},{3,1},{4,6},{6,4},{5,7},{7,5},{8,10},{10,8},{9,1... | collective-permute-start | bytes 786440 | tf_op jit(solution)/shard_map/ppermute | solution.py:45
  38.7 28.1 %collective-permute-start.4 = (bf16[64,1536]{1,0:T(8,128)(2,1)S(1)}, bf16[64,1536]{1,0:T(8,128)(2,1)S(1)}, u32[]{:S(2)}, u32[]{:S(2)}) collective-permute-start(bf16[64,1536]{1,0:T(8,128)(2,1)S(1)} %slice.200), channel_id=1, source_target_pairs={{0,8},{8,16},{16,24},{24,0},{1,9},{9,17},{17,25},{25,1},{2,10},{10... | collective-permute-start | bytes 589832 | tf_op jit(solution)/shard_map/ppermute | solution.py:45
  38.8 11.0 %collective-permute-start.16 = (bf16[64,512]{1,0:T(8,128)(2,1)S(1)}, bf16[64,512]{1,0:T(8,128)(2,1)S(1)}, u32[]{:S(2)}, u32[]{:S(2)}) collective-permute-start(bf16[64,512]{1,0:T(8,128)(2,1)S(1)} %slice.209), channel_id=1, source_target_pairs={{0,8},{8,16},{16,24},{24,0},{1,9},{9,17},{17,25},{25,1},{2,10},{10... | collective-permute-start | bytes 196616 | tf_op jit(solution)/shard_map/ppermute | solution.py:45
  39.9 41.8 %collective-permute-start.28 = (bf16[2,128,1024]{2,1,0:T(8,128)(2,1)S(1)}, bf16[2,128,1024]{2,1,0:T(8,128)(2,1)}, u32[]{:S(2)}, u32[]{:S(2)}) collective-permute-start(bf16[2,128,1024]{2,1,0:T(8,128)(2,1)S(1)} %bitcast_dynamic-update-slice_fusion.21), channel_id=1, source_target_pairs={{0,8},{8,16},{16,24},{24,0},{1,9},{9,17},{17,25},{25,1},{2,10},{10... | collective-permute-start | bytes 1572872 | tf_op jit(solution)/shard_map/ppermute | solution.py:45
  49.8 8.8 %collective-permute-start.17 = (bf16[64,512]{1,0:T(8,128)(2,1)S(1)}, bf16[64,512]{1,0:T(8,128)(2,1)S(1)}, u32[]{:S(2)}, u32[]{:S(2)}) collective-permute-start(bf16[64,512]{1,0:T(8,128)(2,1)S(1)} %collective-permute-done.16), channel_id=1, source_target_pairs={{0,8},{8,16},{16,24},{24,0},{1,9},{9,17},{17,25},{25,1},{2,10},{10... | collective-permute-start | bytes 196616 | tf_op jit(solution)/shard_map/ppermute | solution.py:45
  58.6 11.5 %collective-permute-start.22 = (bf16[64,2048]{1,0:T(8,128)(2,1)S(1)}, bf16[64,2048]{1,0:T(8,128)(2,1)S(1)}, u32[]{:S(2)}, u32[]{:S(2)}) collective-permute-start(bf16[64,2048]{1,0:T(8,128)(2,1)S(1)} %slice.210), channel_id=1, source_target_pairs={{0,4},{4,0},{1,5},{5,1},{2,6},{6,2},{3,7},{7,3},{8,12},{12,8},{9,1... | collective-permute-start | bytes 786440 | tf_op jit(solution)/shard_map/ppermute | solution.py:45
  60.1 6.1 %collective-permute-start.18 = (bf16[64,512]{1,0:T(8,128)(2,1)S(1)}, bf16[64,512]{1,0:T(8,128)(2,1)S(1)}, u32[]{:S(2)}, u32[]{:S(2)}) collective-permute-start(bf16[64,512]{1,0:T(8,128)(2,1)S(1)} %collective-permute-done.17), channel_id=1, source_target_pairs={{0,8},{8,16},{16,24},{24,0},{1,9},{9,17},{17,25},{25,1},{2,10},{10... | collective-permute-start | bytes 196616 | tf_op jit(solution)/shard_map/ppermute | solution.py:45
  66.2 32.1 %collective-permute-start.13 = (bf16[4,2,32,1024]{3,2,1,0:T(8,128)(2,1)S(1)}, bf16[4,2,32,1024]{3,2,1,0:T(8,128)(2,1)S(1)}, u32[]{:S(2)}, u32[]{:S(2)}) collective-permute-start(bf16[4,2,32,1024]{3,2,1,0:T(8,128)(2,1)S(1)} %bitcast_dynamic-update-slice_fusion.27), channel_id=1, source_target_pairs={{0,4},{4,0},{1,5},{5,1},{2,6},{6,2},{3,7},{7,3},{8,12},{12,8},{9,1... | collective-permute-start | bytes 1572872 | tf_op jit(solution)/shard_map/ppermute | solution.py:45
  66.8 13.0 %collective-permute-start.19 = (bf16[4,64,512]{2,1,0:T(8,128)(2,1)S(1)}, bf16[4,64,512]{2,1,0:T(8,128)(2,1)S(1)}, u32[]{:S(2)}, u32[]{:S(2)}) collective-permute-start(bf16[4,64,512]{2,1,0:T(8,128)(2,1)S(1)} %bitcast_dynamic-update-slice_fusion.33), channel_id=1, source_target_pairs={{0,2},{2,0},{1,3},{3,1},{4,6},{6,4},{5,7},{7,5},{8,10},{10,8},{9,1... | collective-permute-start | bytes 786440 | tf_op jit(solution)/shard_map/ppermute | solution.py:45
  70.1 9.6 %collective-permute-start.5 = (bf16[64,1536]{1,0:T(8,128)(2,1)S(1)}, bf16[64,1536]{1,0:T(8,128)(2,1)S(1)}, u32[]{:S(2)}, u32[]{:S(2)}) collective-permute-start(bf16[64,1536]{1,0:T(8,128)(2,1)S(1)} %collective-permute-done.4), channel_id=1, source_target_pairs={{0,8},{8,16},{16,24},{24,0},{1,9},{9,17},{17,25},{25,1},{2,10},{10... | collective-permute-start | bytes 589832 | tf_op jit(solution)/shard_map/ppermute | solution.py:45
  79.7 28.5 %collective-permute-start.23 = (bf16[2,64,2048]{2,1,0:T(8,128)(2,1)S(1)}, bf16[2,64,2048]{2,1,0:T(8,128)(2,1)}, u32[]{:S(2)}, u32[]{:S(2)}) collective-permute-start(bf16[2,64,2048]{2,1,0:T(8,128)(2,1)S(1)} %bitcast_dynamic-update-slice_fusion.23), channel_id=1, source_target_pairs={{0,8},{8,16},{16,24},{24,0},{1,9},{9,17},{17,25},{25,1},{2,10},{10... | collective-permute-start | bytes 1572872 | tf_op jit(solution)/shard_map/ppermute | solution.py:45
  79.8 16.3 %collective-permute-start.6 = (bf16[64,1536]{1,0:T(8,128)(2,1)S(1)}, bf16[64,1536]{1,0:T(8,128)(2,1)S(1)}, u32[]{:S(2)}, u32[]{:S(2)}) collective-permute-start(bf16[64,1536]{1,0:T(8,128)(2,1)S(1)} %collective-permute-done.5), channel_id=1, source_target_pairs={{0,8},{8,16},{16,24},{24,0},{1,9},{9,17},{17,25},{25,1},{2,10},{10... | collective-permute-start | bytes 589832 | tf_op jit(solution)/shard_map/ppermute | solution.py:45
  81.8 38.3 %collective-permute-start.20 = (bf16[4,2,64,512]{3,2,1,0:T(8,128)(2,1)}, bf16[4,2,64,512]{3,2,1,0:T(8,128)(2,1)}, u32[]{:S(2)}, u32[]{:S(2)}) collective-permute-start(bf16[4,2,64,512]{3,2,1,0:T(8,128)(2,1)} %bitcast_dynamic-update-slice_fusion.25), channel_id=1, source_target_pairs={{0,4},{4,0},{1,5},{5,1},{2,6},{6,2},{3,7},{7,3},{8,12},{12,8},{9,1... | collective-permute-start | bytes 1572872 | tf_op jit(solution)/shard_map/ppermute | solution.py:45
  96.1 25.1 %collective-permute-start.29 = (bf16[2,128,1024]{2,1,0:T(8,128)(2,1)}, bf16[2,128,1024]{2,1,0:T(8,128)(2,1)}, u32[]{:S(2)}, u32[]{:S(2)}) collective-permute-start(bf16[2,128,1024]{2,1,0:T(8,128)(2,1)} %collective-permute-done.28), channel_id=1, source_target_pairs={{0,8},{8,16},{16,24},{24,0},{1,9},{9,17},{17,25},{25,1},{2,10},{10... | collective-permute-start | bytes 1572872 | tf_op jit(solution)/shard_map/ppermute | solution.py:45
  98.3 14.4 %collective-permute-start.7 = (bf16[4,64,1536]{2,1,0:T(8,128)(2,1)S(1)}, bf16[4,64,1536]{2,1,0:T(8,128)(2,1)S(1)}, u32[]{:S(2)}, u32[]{:S(2)}) collective-permute-start(bf16[4,64,1536]{2,1,0:T(8,128)(2,1)S(1)} %bitcast_dynamic-update-slice_fusion.28), channel_id=1, source_target_pairs={{0,4},{4,0},{1,5},{5,1},{2,6},{6,2},{3,7},{7,3},{8,12},{12,8},{9,1... | collective-permute-start | bytes 2359304 | tf_op jit(solution)/shard_map/ppermute | solution.py:45
  103.4 7.9 %collective-permute-start.1 = (bf16[2,1,1024]{2,1,0:T(2,128)(2,1)S(1)}, bf16[2,1,1024]{2,1,0:T(2,128)(2,1)S(1)}, u32[]{:S(2)}, u32[]{:S(2)}) collective-permute-start(bf16[2,1,1024]{2,1,0:T(2,128)(2,1)S(1)} %slice_bitcast_fusion.3), channel_id=1, source_target_pairs={{0,4},{4,8},{8,12},{12,16},{16,20},{20,24},{24,28},{1,5},{5,9},{9,... | collective-permute-start | bytes 12296 | tf_op jit(solution)/shard_map/ppermute | solution.py:30
  108.3 17.2 %collective-permute-start.24 = (bf16[2,64,2048]{2,1,0:T(8,128)(2,1)}, bf16[2,64,2048]{2,1,0:T(8,128)(2,1)}, u32[]{:S(2)}, u32[]{:S(2)}) collective-permute-start(bf16[2,64,2048]{2,1,0:T(8,128)(2,1)} %collective-permute-done.23), channel_id=1, source_target_pairs={{0,8},{8,16},{16,24},{24,0},{1,9},{9,17},{17,25},{25,1},{2,10},{10... | collective-permute-start | bytes 1572872 | tf_op jit(solution)/shard_map/ppermute | solution.py:45
  113.7 24.9 %collective-permute-start.8 = (bf16[4,2,64,1536]{3,2,1,0:T(8,128)(2,1)}, bf16[4,2,64,1536]{3,2,1,0:T(8,128)(2,1)}, u32[]{:S(2)}, u32[]{:S(2)}) collective-permute-start(bf16[4,2,64,1536]{3,2,1,0:T(8,128)(2,1)} %bitcast_dynamic-update-slice_fusion.7), channel_id=1, source_target_pairs={{0,2},{2,0},{1,3},{3,1},{4,6},{6,4},{5,7},{7,5},{8,10},{10,8},{9,1... | collective-permute-start | bytes 4718600 | tf_op jit(solution)/shard_map/ppermute | solution.py:45
  121.2 15.2 %collective-permute-start.30 = (bf16[2,128,1024]{2,1,0:T(8,128)(2,1)}, bf16[2,128,1024]{2,1,0:T(8,128)(2,1)S(1)}, u32[]{:S(2)}, u32[]{:S(2)}) collective-permute-start(bf16[2,128,1024]{2,1,0:T(8,128)(2,1)} %collective-permute-done.29), channel_id=1, source_target_pairs={{0,8},{8,16},{16,24},{24,0},{1,9},{9,17},{17,25},{25,1},{2,10},{10... | collective-permute-start | bytes 1572872 | tf_op jit(solution)/shard_map/ppermute | solution.py:45
  125.5 56.5 %collective-permute-start.25 = (bf16[2,64,2048]{2,1,0:T(8,128)(2,1)}, bf16[2,64,2048]{2,1,0:T(8,128)(2,1)}, u32[]{:S(2)}, u32[]{:S(2)}) collective-permute-start(bf16[2,64,2048]{2,1,0:T(8,128)(2,1)} %collective-permute-done.24), channel_id=1, source_target_pairs={{0,8},{8,16},{16,24},{24,0},{1,9},{9,17},{17,25},{25,1},{2,10},{10... | collective-permute-start | bytes 1572872 | tf_op jit(solution)/shard_map/ppermute | solution.py:45
  137.2 49.7 %collective-permute-start.31 = (bf16[4,2,128,1024]{3,2,1,0:T(8,128)(2,1)}, bf16[4,2,128,1024]{3,2,1,0:T(8,128)(2,1)}, u32[]{:S(2)}, u32[]{:S(2)}) collective-permute-start(bf16[4,2,128,1024]{3,2,1,0:T(8,128)(2,1)} %bitcast_dynamic-update-slice_fusion.10), channel_id=1, source_target_pairs={{0,4},{4,0},{1,5},{5,1},{2,6},{6,2},{3,7},{7,3},{8,12},{12,8},{9,1... | collective-permute-start | bytes 6291464 | tf_op jit(solution)/shard_map/ppermute | solution.py:45
  143.2 31.2 %all-to-all-start.1 = ((f32[8,2,2,512]{3,2,1,0:T(2,128)}), f32[8,2,2,512]{3,2,1,0:T(2,128)S(1)}, u32[]{:S(2)}, u32[]{:S(2)}) async-start(f32[8,2,2,512]{3,2,1,0:T(2,128)} %broadcast_in_dim.289), calls=%async_computation.1 | async-start | bytes 131072 | tf_op jit(solution)/shard_map/all_to_all | solution.py:323
  177.5 12.8 %collective-permute-start.14 = (f32[512,1024]{1,0:T(8,128)S(1)}, f32[512,1024]{1,0:T(8,128)S(1)}, u32[]{:S(2)}, u32[]{:S(2)}) collective-permute-start(f32[512,1024]{1,0:T(8,128)S(1)} %fusion.96), channel_id=1, source_target_pairs={{0,1},{1,0},{2,3},{3,2},{4,5},{5,4},{6,7},{7,6},{8,9},{9,8},{10,11... | collective-permute-start | bytes 6291464 | tf_op jit(solution)/shard_map/ppermute | solution.py:24
  183.9 48.3 %collective-permute-start.26 = (bf16[4,2,64,2048]{3,2,1,0:T(8,128)(2,1)}, bf16[4,2,64,2048]{3,2,1,0:T(8,128)(2,1)}, u32[]{:S(2)}, u32[]{:S(2)}) collective-permute-start(bf16[4,2,64,2048]{3,2,1,0:T(8,128)(2,1)} %bitcast_dynamic-update-slice_fusion.14), channel_id=1, source_target_pairs={{0,2},{2,0},{1,3},{3,1},{4,6},{6,4},{5,7},{7,5},{8,10},{10,8},{9,1... | collective-permute-start | bytes 6291464 | tf_op jit(solution)/shard_map/ppermute | solution.py:45
  199.8 34.2 %collective-permute-start.15 = (f32[2,1,1024]{2,1,0:T(1,128)S(1)}, f32[2,1,1024]{2,1,0:T(1,128)S(1)}, u32[]{:S(2)}, u32[]{:S(2)}) collective-permute-start(f32[2,1,1024]{2,1,0:T(1,128)S(1)} %slice.207), channel_id=1, source_target_pairs={{0,4},{4,8},{8,12},{12,16},{16,20},{20,24},{24,28},{1,5},{5,9},{9,... | collective-permute-start | bytes 24584 | tf_op jit(solution)/shard_map/ppermute | solution.py:30
  243.4 21.8 %collective-permute-start.32 = (f32[512,1024]{1,0:T(8,128)S(1)}, f32[512,1024]{1,0:T(8,128)S(1)}, u32[]{:S(2)}, u32[]{:S(2)}) collective-permute-start(f32[512,1024]{1,0:T(8,128)S(1)} %fusion.49), channel_id=1, source_target_pairs={{0,1},{1,0},{2,3},{3,2},{4,5},{5,4},{6,7},{7,6},{8,9},{9,8},{10,11... | collective-permute-start | bytes 6291464 | tf_op jit(solution)/shard_map/ppermute | solution.py:24
  254.4 75.7 %collective-permute-start.42 = (bf16[4,2,64,2048]{3,2,1,0:T(8,128)(2,1)}, bf16[4,2,64,2048]{3,2,1,0:T(8,128)(2,1)}, u32[]{:S(2)}, u32[]{:S(2)}) collective-permute-start(bf16[4,2,64,2048]{3,2,1,0:T(8,128)(2,1)} %dynamic-slice_bitcast_fusion.1), channel_id=1, source_target_pairs={{0,2},{2,0},{1,3},{3,1},{4,6},{6,4},{5,7},{7,5},{8,10},{10,8},{9,1... | collective-permute-start | bytes 6291464 | tf_op jit(solution)/shard_map/ppermute | solution.py:68
  262.5 74.1 %collective-permute-start.58 = (bf16[4,2,128,1024]{3,2,1,0:T(8,128)(2,1)}, bf16[4,2,128,1024]{3,2,1,0:T(8,128)(2,1)}, u32[]{:S(2)}, u32[]{:S(2)}) collective-permute-start(bf16[4,2,128,1024]{3,2,1,0:T(8,128)(2,1)} %dynamic-slice_bitcast_fusion), channel_id=1, source_target_pairs={{0,4},{4,0},{1,5},{5,1},{2,6},{6,2},{3,7},{7,3},{8,12},{12,8},{9,1... | collective-permute-start | bytes 6291464 | tf_op jit(solution)/shard_map/ppermute | solution.py:68
  270.4 51.0 %collective-permute-start.47 = (bf16[4,2,64,512]{3,2,0,1:T(8,128)(2,1)}, bf16[4,2,64,512]{3,2,0,1:T(8,128)(2,1)}, u32[]{:S(2)}, u32[]{:S(2)}) collective-permute-start(bf16[4,2,64,512]{3,2,0,1:T(8,128)(2,1)} %bitcast.502), channel_id=1, source_target_pairs={{0,4},{4,0},{1,5},{5,1},{2,6},{6,2},{3,7},{7,3},{8,12},{12,8},{9,1... | collective-permute-start | bytes 1572872 | tf_op jit(solution)/shard_map/ppermute | solution.py:68
  276.1 48.1 %collective-permute-start.33 = (f32[2,1,1024]{2,1,0:T(1,128)S(1)}, f32[2,1,1024]{2,1,0:T(1,128)S(1)}, u32[]{:S(2)}, u32[]{:S(2)}) collective-permute-start(f32[2,1,1024]{2,1,0:T(1,128)S(1)} %slice_multiply_fusion.2), channel_id=1, source_target_pairs={{4,0},{8,4},{12,8},{16,12},{20,16},{24,20},{28,24},{5,1},{9,5},{13... | collective-permute-start | bytes 24584 | tf_op jit(solution)/shard_map/ppermute | solution.py:30
  322.7 7.0 %collective-permute-start.48 = (bf16[4,64,512]{2,1,0:T(8,128)(2,1)S(1)}, bf16[4,64,512]{2,1,0:T(8,128)(2,1)S(1)}, u32[]{:S(2)}, u32[]{:S(2)}) collective-permute-start(bf16[4,64,512]{2,1,0:T(8,128)(2,1)S(1)} %fusion.58), channel_id=1, source_target_pairs={{0,2},{2,0},{1,3},{3,1},{4,6},{6,4},{5,7},{7,5},{8,10},{10,8},{9,1... | collective-permute-start | bytes 786440 | tf_op jit(solution)/shard_map/ppermute | solution.py:68
  326.7 61.2 %collective-permute-start.34 = (f32[2,256,1024]{2,1,0:T(8,128)S(1)}, f32[2,256,1024]{2,1,0:T(8,128)S(1)}, u32[]{:S(2)}, u32[]{:S(2)}) collective-permute-start(f32[2,256,1024]{2,1,0:T(8,128)S(1)} %maximum_add_fusion), channel_id=1, source_target_pairs={{0,1},{1,0},{2,3},{3,2},{4,5},{5,4},{6,7},{7,6},{8,9},{9,8},{10,11... | collective-permute-start | bytes 6291464 | tf_op jit(solution)/shard_map/ppermute | solution.py:24
  329.8 6.7 %collective-permute-start.49 = (bf16[64,512]{1,0:T(8,128)(2,1)S(1)}, bf16[64,512]{1,0:T(8,128)(2,1)S(1)}, u32[]{:S(2)}, u32[]{:S(2)}) collective-permute-start(bf16[64,512]{1,0:T(8,128)(2,1)S(1)} %fusion.67), channel_id=1, source_target_pairs={{0,8},{8,16},{16,24},{24,0},{1,9},{9,17},{17,25},{25,1},{2,10},{10... | collective-permute-start | bytes 196616 | tf_op jit(solution)/shard_map/ppermute | solution.py:68
  332.8 16.7 %collective-permute-start.43 = (bf16[2,64,2048]{2,1,0:T(8,128)(2,1)S(1)}, bf16[2,64,2048]{2,1,0:T(8,128)(2,1)S(1)}, u32[]{:S(2)}, u32[]{:S(2)}) collective-permute-start(bf16[2,64,2048]{2,1,0:T(8,128)(2,1)S(1)} %fusion.50), channel_id=1, source_target_pairs={{0,8},{8,16},{16,24},{24,0},{1,9},{9,17},{17,25},{25,1},{2,10},{10... | collective-permute-start | bytes 1572872 | tf_op jit(solution)/shard_map/ppermute | solution.py:68
  336.6 14.4 %collective-permute-start.50 = (bf16[64,512]{1,0:T(8,128)(2,1)S(1)}, bf16[64,512]{1,0:T(8,128)(2,1)S(1)}, u32[]{:S(2)}, u32[]{:S(2)}) collective-permute-start(bf16[64,512]{1,0:T(8,128)(2,1)S(1)} %fusion.66), channel_id=1, source_target_pairs={{0,8},{8,16},{16,24},{24,0},{1,9},{9,17},{17,25},{25,1},{2,10},{10... | collective-permute-start | bytes 196616 | tf_op jit(solution)/shard_map/ppermute | solution.py:68
  339.3 22.9 %collective-permute-start.59 = (bf16[2,128,1024]{2,1,0:T(8,128)(2,1)S(1)}, bf16[2,128,1024]{2,1,0:T(8,128)(2,1)S(1)}, u32[]{:S(2)}, u32[]{:S(2)}) collective-permute-start(bf16[2,128,1024]{2,1,0:T(8,128)(2,1)S(1)} %fusion.51), channel_id=1, source_target_pairs={{0,8},{8,16},{16,24},{24,0},{1,9},{9,17},{17,25},{25,1},{2,10},{10... | collective-permute-start | bytes 1572872 | tf_op jit(solution)/shard_map/ppermute | solution.py:68
  349.6 25.2 %collective-permute-start.44 = (bf16[2,64,2048]{2,1,0:T(8,128)(2,1)S(1)}, bf16[2,64,2048]{2,1,0:T(8,128)(2,1)S(1)}, u32[]{:S(2)}, u32[]{:S(2)}) collective-permute-start(bf16[2,64,2048]{2,1,0:T(8,128)(2,1)S(1)} %fusion.32), channel_id=1, source_target_pairs={{0,8},{8,16},{16,24},{24,0},{1,9},{9,17},{17,25},{25,1},{2,10},{10... | collective-permute-start | bytes 1572872 | tf_op jit(solution)/shard_map/ppermute | solution.py:68
  350.9 23.9 %collective-permute-start.51 = (bf16[64,512]{1,0:T(8,128)(2,1)S(1)}, bf16[64,512]{1,0:T(8,128)(2,1)S(1)}, u32[]{:S(2)}, u32[]{:S(2)}) collective-permute-start(bf16[64,512]{1,0:T(8,128)(2,1)S(1)} %fusion.65), channel_id=1, source_target_pairs={{0,8},{8,16},{16,24},{24,0},{1,9},{9,17},{17,25},{25,1},{2,10},{10... | collective-permute-start | bytes 196616 | tf_op jit(solution)/shard_map/ppermute | solution.py:68
  362.3 23.7 %collective-permute-start.60 = (bf16[2,128,1024]{2,1,0:T(8,128)(2,1)S(1)}, bf16[2,128,1024]{2,1,0:T(8,128)(2,1)S(1)}, u32[]{:S(2)}, u32[]{:S(2)}) collective-permute-start(bf16[2,128,1024]{2,1,0:T(8,128)(2,1)S(1)} %fusion.30), channel_id=1, source_target_pairs={{0,8},{8,16},{16,24},{24,0},{1,9},{9,17},{17,25},{25,1},{2,10},{10... | collective-permute-start | bytes 1572872 | tf_op jit(solution)/shard_map/ppermute | solution.py:68
  375.8 59.2 %collective-permute-start.45 = (bf16[2,64,2048]{2,1,0:T(8,128)(2,1)}, bf16[2,64,2048]{2,1,0:T(8,128)(2,1)}, u32[]{:S(2)}, u32[]{:S(2)}) collective-permute-start(bf16[2,64,2048]{2,1,0:T(8,128)(2,1)} %fusion.31), channel_id=1, source_target_pairs={{0,8},{8,16},{16,24},{24,0},{1,9},{9,17},{17,25},{25,1},{2,10},{10... | collective-permute-start | bytes 1572872 | tf_op jit(solution)/shard_map/ppermute | solution.py:68
  387.0 54.3 %collective-permute-start.61 = (bf16[2,128,1024]{2,1,0:T(8,128)(2,1)}, bf16[2,128,1024]{2,1,0:T(8,128)(2,1)}, u32[]{:S(2)}, u32[]{:S(2)}) collective-permute-start(bf16[2,128,1024]{2,1,0:T(8,128)(2,1)} %fusion.29), channel_id=1, source_target_pairs={{0,8},{8,16},{16,24},{24,0},{1,9},{9,17},{17,25},{25,1},{2,10},{10... | collective-permute-start | bytes 1572872 | tf_op jit(solution)/shard_map/ppermute | solution.py:68
  397.1 13.8 %all-to-all-start.2 = ((f32[8,2,2,512]{3,2,1,0:T(2,128)}), f32[8,2,2,512]{3,2,1,0:T(2,128)S(1)}, u32[]{:S(2)}, u32[]{:S(2)}) async-start(f32[8,2,2,512]{3,2,1,0:T(2,128)} %broadcast_in_dim.335), calls=%async_computation.2 | async-start | bytes 131072 | tf_op jit(solution)/shard_map/all_to_all | solution.py:323
  406.1 33.3 %collective-permute-start.53 = (bf16[4,2,32,1024]{3,2,0,1:T(8,128)(2,1)}, bf16[4,2,32,1024]{3,2,0,1:T(8,128)(2,1)}, u32[]{:S(2)}, u32[]{:S(2)}) collective-permute-start(bf16[4,2,32,1024]{3,2,0,1:T(8,128)(2,1)} %bitcast.501), channel_id=1, source_target_pairs={{0,4},{4,0},{1,5},{5,1},{2,6},{6,2},{3,7},{7,3},{8,12},{12,8},{9,1... | collective-permute-start | bytes 1572872 | tf_op jit(solution)/shard_map/ppermute | solution.py:68
  422.3 8.6 %collective-permute-start.35 = (f32[2,1,1024]{2,1,0:T(1,128)S(1)}, f32[2,1,1024]{2,1,0:T(1,128)S(1)}, u32[]{:S(2)}, u32[]{:S(2)}) collective-permute-start(f32[2,1,1024]{2,1,0:T(1,128)S(1)} %slice_multiply_fusion.1), channel_id=1, source_target_pairs={{4,0},{8,4},{12,8},{16,12},{20,16},{24,20},{28,24},{5,1},{9,5},{13... | collective-permute-start | bytes 24584 | tf_op jit(solution)/shard_map/ppermute | solution.py:30
  429.4 58.0 %collective-permute-start.37 = (bf16[4,2,64,1536]{3,2,1,0:T(8,128)(2,1)}, bf16[4,2,64,1536]{3,2,1,0:T(8,128)(2,1)}, u32[]{:S(2)}, u32[]{:S(2)}) collective-permute-start(bf16[4,2,64,1536]{3,2,1,0:T(8,128)(2,1)} %dynamic-slice_bitcast_fusion.2), channel_id=1, source_target_pairs={{0,2},{2,0},{1,3},{3,1},{4,6},{6,4},{5,7},{7,5},{8,10},{10,8},{9,1... | collective-permute-start | bytes 4718600 | tf_op jit(solution)/shard_map/ppermute | solution.py:68
  434.9 51.8 %collective-permute-start.36 = (f32[256,1024]{1,0:T(8,128)S(1)}, f32[256,1024]{1,0:T(8,128)S(1)}, u32[]{:S(2)}, u32[]{:S(2)}) collective-permute-start(f32[256,1024]{1,0:T(8,128)S(1)} %dynamic-slice_bitcast_fusion.3), channel_id=1, source_target_pairs={{0,1},{1,0},{2,3},{3,2},{4,5},{5,4},{6,7},{7,6},{8,9},{9,8},{10,11... | collective-permute-start | bytes 3145736 | tf_op jit(solution)/shard_map/ppermute | solution.py:24
  436.6 39.3 %collective-permute-start.46 = (bf16[64,2048]{1,0:T(8,128)(2,1)S(1)}, bf16[64,2048]{1,0:T(8,128)(2,1)S(1)}, u32[]{:S(2)}, u32[]{:S(2)}) collective-permute-start(bf16[64,2048]{1,0:T(8,128)(2,1)S(1)} %fusion.57), channel_id=1, source_target_pairs={{0,4},{4,0},{1,5},{5,1},{2,6},{6,2},{3,7},{7,3},{8,12},{12,8},{9,1... | collective-permute-start | bytes 786440 | tf_op jit(solution)/shard_map/ppermute | solution.py:68
  440.6 26.6 %collective-permute-start.54 = (bf16[4,32,1024]{2,1,0:T(8,128)(2,1)S(1)}, bf16[4,32,1024]{2,1,0:T(8,128)(2,1)S(1)}, u32[]{:S(2)}, u32[]{:S(2)}) collective-permute-start(bf16[4,32,1024]{2,1,0:T(8,128)(2,1)S(1)} %fusion.59), channel_id=1, source_target_pairs={{0,2},{2,0},{1,3},{3,1},{4,6},{6,4},{5,7},{7,5},{8,10},{10,8},{9,1... | collective-permute-start | bytes 786440 | tf_op jit(solution)/shard_map/ppermute | solution.py:68
  467.3 6.2 %collective-permute-start.55 = (bf16[32,1024]{1,0:T(8,128)(2,1)S(1)}, bf16[32,1024]{1,0:T(8,128)(2,1)S(1)}, u32[]{:S(2)}, u32[]{:S(2)}) collective-permute-start(bf16[32,1024]{1,0:T(8,128)(2,1)S(1)} %fusion.68), channel_id=1, source_target_pairs={{0,8},{8,16},{16,24},{24,0},{1,9},{9,17},{17,25},{25,1},{2,10},{10... | collective-permute-start | bytes 196616 | tf_op jit(solution)/shard_map/ppermute | solution.py:68
  471.6 8.9 %collective-permute-start.62 = (bf16[128,1024]{1,0:T(8,128)(2,1)S(1)}, bf16[128,1024]{1,0:T(8,128)(2,1)S(1)}, u32[]{:S(2)}, u32[]{:S(2)}) collective-permute-start(bf16[128,1024]{1,0:T(8,128)(2,1)S(1)} %fusion.60), channel_id=1, source_target_pairs={{0,2},{2,0},{1,3},{3,1},{4,6},{6,4},{5,7},{7,5},{8,10},{10,8},{9,1... | collective-permute-start | bytes 786440 | tf_op jit(solution)/shard_map/ppermute | solution.py:68
  473.5 6.1 %collective-permute-start.56 = (bf16[32,1024]{1,0:T(8,128)(2,1)S(1)}, bf16[32,1024]{1,0:T(8,128)(2,1)S(1)}, u32[]{:S(2)}, u32[]{:S(2)}) collective-permute-start(bf16[32,1024]{1,0:T(8,128)(2,1)S(1)} %fusion.64), channel_id=1, source_target_pairs={{0,8},{8,16},{16,24},{24,0},{1,9},{9,17},{17,25},{25,1},{2,10},{10... | collective-permute-start | bytes 196616 | tf_op jit(solution)/shard_map/ppermute | solution.py:68
  479.7 6.4 %collective-permute-start.57 = (bf16[32,1024]{1,0:T(8,128)(2,1)S(1)}, bf16[32,1024]{1,0:T(8,128)(2,1)S(1)}, u32[]{:S(2)}, u32[]{:S(2)}) collective-permute-start(bf16[32,1024]{1,0:T(8,128)(2,1)S(1)} %fusion.63), channel_id=1, source_target_pairs={{0,8},{8,16},{16,24},{24,0},{1,9},{9,17},{17,25},{25,1},{2,10},{10... | collective-permute-start | bytes 196616 | tf_op jit(solution)/shard_map/ppermute | solution.py:68
  489.8 14.3 %collective-permute-start.38 = (bf16[4,64,1536]{2,1,0:T(8,128)(2,1)S(1)}, bf16[4,64,1536]{2,1,0:T(8,128)(2,1)S(1)}, u32[]{:S(2)}, u32[]{:S(2)}) collective-permute-start(bf16[4,64,1536]{2,1,0:T(8,128)(2,1)S(1)} %fusion.48), channel_id=1, source_target_pairs={{0,4},{4,0},{1,5},{5,1},{2,6},{6,2},{3,7},{7,3},{8,12},{12,8},{9,1... | collective-permute-start | bytes 2359304 | tf_op jit(solution)/shard_map/ppermute | solution.py:68
  504.4 9.5 %collective-permute-start.39 = (bf16[64,1536]{1,0:T(8,128)(2,1)S(1)}, bf16[64,1536]{1,0:T(8,128)(2,1)S(1)}, u32[]{:S(2)}, u32[]{:S(2)}) collective-permute-start(bf16[64,1536]{1,0:T(8,128)(2,1)S(1)} %fusion.61), channel_id=1, source_target_pairs={{0,8},{8,16},{16,24},{24,0},{1,9},{9,17},{17,25},{25,1},{2,10},{10... | collective-permute-start | bytes 589832 | tf_op jit(solution)/shard_map/ppermute | solution.py:68
  514.0 7.5 %collective-permute-start.40 = (bf16[64,1536]{1,0:T(8,128)(2,1)S(1)}, bf16[64,1536]{1,0:T(8,128)(2,1)S(1)}, u32[]{:S(2)}, u32[]{:S(2)}) collective-permute-start(bf16[64,1536]{1,0:T(8,128)(2,1)S(1)} %fusion.56), channel_id=1, source_target_pairs={{0,8},{8,16},{16,24},{24,0},{1,9},{9,17},{17,25},{25,1},{2,10},{10... | collective-permute-start | bytes 589832 | tf_op jit(solution)/shard_map/ppermute | solution.py:68
  521.6 7.5 %collective-permute-start.41 = (bf16[64,1536]{1,0:T(8,128)(2,1)S(1)}, bf16[64,1536]{1,0:T(8,128)(2,1)S(1)}, u32[]{:S(2)}, u32[]{:S(2)}) collective-permute-start(bf16[64,1536]{1,0:T(8,128)(2,1)S(1)} %fusion.55), channel_id=1, source_target_pairs={{0,8},{8,16},{16,24},{24,0},{1,9},{9,17},{17,25},{25,1},{2,10},{10... | collective-permute-start | bytes 589832 | tf_op jit(solution)/shard_map/ppermute | solution.py:68
  531.1 13.6 %collective-permute-start.52 = (f32[32,4096]{1,0:T(8,128)}, f32[32,4096]{1,0:T(8,128)}, u32[]{:S(2)}, u32[]{:S(2)}) collective-permute-start(f32[32,4096]{1,0:T(8,128)} %dynamic-slice_bitcast_fusion.4), channel_id=1, source_target_pairs={{0,1},{1,0},{2,3},{3,2},{4,5},{5,4},{6,7},{7,6},{8,9},{9,8},{10,11... | collective-permute-start | bytes 1572872 | tf_op jit(solution)/shard_map/ppermute | solution.py:24
  532.0 10.8 %all-to-all-start.3 = ((f32[32,1,352]{2,1,0:T(1,128)}), f32[32,1,352]{2,1,0:T(1,128)S(1)}, u32[]{:S(2)}, u32[]{:S(2)}) async-start(f32[32,1,352]{2,1,0:T(1,128)} %reshape.897), calls=%async_computation.3 | async-start | bytes 98304 | tf_op jit(solution)/shard_map/all_to_all | solution.py:448
  (77 other events, 553.8 us)
